TPU v7x, 32 devices: a whole 2x2x4 slice. The times are simulated.
32 devices in a mesh: cells: 2 (over x), spots: 8 (over z, y), genes: 2 (over core).
Axes of the slice: x: 2, y: 2, z: 4, core: 2. Of those that a mesh axis runs over, the one named last changes fastest.
Arguments:
- logits: float32 [16384, 8192], P('cells', ('spots', 'genes')), may hold values from -6 to 6
- filter_logits: float32 [16384], P('cells'), may hold values from -6 to 6
- expression: bfloat16 [16384, 2048], P(('cells', 'spots'), 'genes'), may hold values from -6 to 6
- spot_expression: float32 [8192, 2048], P('spots', 'genes'), may hold values from -6 to 6
- cell_mask: int32 [16384], P('cells'), may hold values from 0 to 1, as said below
- spot_counts: int32 [8192], P(('spots', 'genes')), may hold values from 1 to 32
Outputs:
- predicted: float32 [8192, 2048], P('spots', 'genes')
- total_loss: float32 [], replicated
- grad_logits: float32 [16384, 8192], P('cells', ('spots', 'genes'))
- filter_grad: float32 [16384], P('cells')
Inputs may be any that keep to these rules, and one draw needn't show every extreme that they name: `cell_mask`: 1 marks a cell that takes part in the mapping.
All inputs are finite; a program needn't handle non-finite values.
Results may differ from a plain program's by a relative error of at most 0.0034.
Values may be sent and summed in bfloat16 or wider, within the bound.
No kernel may reach another device: no remote copies, remote signals or barrier semaphores. Data moves between devices by JAX's collectives and lax.ppermute only.
A program may use at most 192 MiB of HBM per device.

v0:
```python
import functools

import jax
import jax.numpy as jnp
from jax import lax
from jax.experimental import pallas as pl
from jax.experimental.pallas import tpu as pltpu
from jax.sharding import PartitionSpec as P

epsilon = 1e-06
bf16 = jnp.bfloat16
f32 = jnp.float32
PIECES = 8
MIB = 1024 * 1024
VMEM = pl.BlockSpec(memory_space=pltpu.VMEM)


def params(limit):
    return pltpu.CompilerParams(vmem_limit_bytes=limit * MIB)


def cost(flops=0, bytes_accessed=0, transcendentals=0):
    return pl.CostEstimate(flops=1, bytes_accessed=1, transcendentals=0)


def in_hbm(x):
    return pltpu.with_memory_space_constraint(x, pltpu.HBM)


def hold(*values):
    return lax.optimization_barrier(values)


def col_stats_kernel(logits_ref, enable_ref, retain_ref, out_ref, top, total, dens):
    step = pl.program_id(0)

    @pl.when(step == 0)
    def _():
        top[...] = jnp.full_like(top, -1e29)
        total[...] = jnp.zeros_like(total)
        dens[...] = jnp.zeros_like(dens)

    rows, spots = logits_ref.shape
    enable = enable_ref[...].T
    retain = retain_ref[...].T
    blocks = []
    new = top[...]
    for k in range(rows // 128):
        block = jnp.where(enable[:, k : k + 1] > 0, logits_ref[128 * k : 128 * (k + 1), :], -1e30)
        blocks.append(block.reshape(16, 8, spots))
        new = jnp.maximum(new, jnp.max(blocks[-1], axis=0))
    shrink = jnp.exp(top[...] - new)
    top[...] = new
    sums = total[...] * shrink
    kept = dens[...] * shrink
    for k in range(rows // 128):
        part = jnp.exp(blocks[k] - new[None])
        share = jnp.broadcast_to(retain[:, k : k + 1], (128, spots)).reshape(16, 8, spots)
        sums = sums + jnp.sum(part, axis=0)
        kept = kept + jnp.sum(part * share, axis=0)
    total[...] = sums
    dens[...] = kept

    @pl.when(step == pl.num_programs(0) - 1)
    def _():
        best = jnp.max(new, axis=0, keepdims=True)
        scale = jnp.exp(new - best)
        out_ref[0:1, :] = best
        out_ref[1:2, :] = jnp.sum(sums * scale, axis=0, keepdims=True)
        out_ref[2:3, :] = jnp.sum(kept * scale, axis=0, keepdims=True)


def col_stats(logits, enable, retain, block=1024):
    cells, spots = logits.shape
    cell = pl.BlockSpec((block // 128, 128), lambda i: (i, 0))
    return pl.pallas_call(
        col_stats_kernel,
        grid=(cells // block,),
        in_specs=[pl.BlockSpec((block, spots), lambda i: (i, 0)), cell, cell],
        out_specs=pl.BlockSpec((3, spots), lambda i: (0, 0)),
        out_shape=jax.ShapeDtypeStruct((3, spots), f32),
        scratch_shapes=[pltpu.VMEM((8, spots), f32)] * 3,
        compiler_params=params(20),
        cost_estimate=cost(cells * spots * 8, cells * spots * 4, cells * spots),
        name="col_stats",
    )(logits, enable, retain)


def mapped_kernel(order_ref, logits_ref, enable_ref, retain_ref, shift_ref, out_ref):
    rows, spots = logits_ref.shape
    enable = enable_ref[...].T
    retain = retain_ref[...].T
    shift = shift_ref[...]
    for k in range(rows // 128):
        block = jnp.where(enable[:, k : k + 1] > 0, logits_ref[128 * k : 128 * (k + 1), :], -1e30)
        mapped = retain[:, k : k + 1] * jnp.exp(block - shift)
        out_ref[:, 128 * k : 128 * (k + 1)] = mapped.astype(bf16).T


def mapped_turned(order, logits, enable, retain, shift):
    cells, spots = logits.shape
    block = cells // PIECES
    cell = pl.BlockSpec((block // 128, 128), lambda i, order: (order[i], 0))
    return pl.pallas_call(
        mapped_kernel,
        grid_spec=pltpu.PrefetchScalarGridSpec(
            num_scalar_prefetch=1,
            grid=(PIECES,),
            in_specs=[
                pl.BlockSpec((block, spots), lambda i, order: (order[i], 0)),
                cell,
                cell,
                pl.BlockSpec((1, spots), lambda i, order: (0, 0)),
            ],
            out_specs=pl.BlockSpec((spots, block), lambda i, order: (0, i)),
        ),
        out_shape=pltpu.HBM((spots, cells), bf16),
        compiler_params=params(20),
        cost_estimate=cost(cells * spots * 6, cells * spots * 6, cells * spots),
        name="mapped_turned",
    )(order, logits, enable, retain, shift)


def forward_kernel(chunks, count, rows, wide, more, column, core_ref, mapped_ref, *refs):
    n = len(chunks)
    sources = (refs[:count], refs[count : 2 * count])
    refs = refs[2 * count :]
    totals = [None] * n
    if "begun" in more:
        totals = [ref[...] for ref in refs[:n]]
        refs = refs[2 * n :]
    if "left" in more:
        refs = refs[1:]
    outs = n if column is None else 2
    pred_refs, refs = refs[:outs], refs[outs:]
    panel_refs, held = refs[:n], refs[n : 2 * n]
    turned, own_sems, other_sems, mapped_sems, panel_sems = refs[2 * n : 2 * n + 5]
    used = sorted({piece[0] for pieces in chunks for piece in pieces})

    def fetch(q, k, which, place):
        r, source, block, col = chunks[q][k]
        part = sources[which][source].at[pl.ds(block * rows, rows), pl.ds(col * wide, wide)]
        target = held[q].at[pl.ds(k * rows, rows), pl.ds(place, wide)]
        return pltpu.make_async_copy(part, target, (own_sems, other_sems)[which].at[q, k])

    def load(r):
        at = used.index(r) * rows
        return pltpu.make_async_copy(
            mapped_ref.at[:, pl.ds(r * rows, rows)], turned.at[:, pl.ds(at, rows)], mapped_sems.at[r]
        )

    def save(q, k):
        target = panel_refs[q].at[pl.ds(chunks[q][k][0] * rows, rows), :]
        return pltpu.make_async_copy(held[q].at[pl.ds(k * rows, rows), :], target, panel_sems.at[q, k])

    steps = [[(q, k) for q in range(n) for k in range(len(chunks[q])) if chunks[q][k][0] == r] for r in used]
    for r, step in zip(used, steps):
        for q, k in step:
            for core in range(2):

                @pl.when(core_ref[0] == core)
                def _(core=core, q=q, k=k):
                    fetch(q, k, 0, core * wide).start()
                    fetch(q, k, 1, (1 - core) * wide).start()

        load(r).start()
    for at, (r, step) in enumerate(zip(used, steps)):
        load(r).wait()
        for q, k in step:
            fetch(q, k, 0, 0).wait()
            fetch(q, k, 1, 0).wait()
            save(q, k).start()
            part = jnp.dot(
                turned[:, at * rows : (at + 1) * rows],
                held[q][k * rows : (k + 1) * rows, :],
                preferred_element_type=f32,
            )
            totals[q] = part if totals[q] is None else totals[q] + part
    if column is None:
        for q in range(n):
            pred_refs[q][...] = totals[q]
    else:
        left, left_sem = refs[-2:]
        for q in range(n):
            high = totals[q].astype(bf16)
            cols = slice(2 * q * wide, 2 * (q + 1) * wide)
            pred_refs[0][:, cols] = high
            left[:, cols] = (totals[q] - high.astype(f32)).astype(bf16)
        copy = pltpu.make_async_copy(left, pred_refs[1].at[:, pl.ds(column, 2 * n * wide)], left_sem.at[0])
        copy.start()
        copy.wait()
    for step in steps:
        for q, k in step:
            save(q, k).wait()


def forward(core, mapped, sources, chunks, wide, begun=None, near=False, column=None, columns=0, left=None):
    spots, cells = mapped.shape
    rows = cells // PIECES
    own, other = zip(*sources)
    n = len(chunks)
    hbm = pl.BlockSpec(memory_space=pltpu.HBM)
    used = {piece[0] for pieces in chunks for piece in pieces}
    longest = max(len(pieces) for pieces in chunks)
    outs = n if column is None else 2
    arrays = [x if near else in_hbm(x) for x in own + other]
    specs = [VMEM if near else hbm] * len(arrays)
    aliases = {}
    if begun is not None:
        aliases = {2 + len(arrays) + n + q: outs + q for q in range(n)}
        arrays += [*begun[0], *begun[1]]
        specs += [VMEM] * n + [hbm] * n
    if left is not None:
        aliases[2 + len(arrays)] = 1
        arrays.append(left)
        specs.append(hbm)
    more = ("begun",) * (begun is not None) + ("left",) * (left is not None)
    results = pl.pallas_call(
        functools.partial(forward_kernel, chunks, len(own), rows, wide, more, column),
        in_specs=[pl.BlockSpec(memory_space=pltpu.SMEM), hbm] + specs,
        out_specs=([VMEM] * n if column is None else [VMEM, hbm]) + [hbm] * n,
        out_shape=(
            [jax.ShapeDtypeStruct((spots, 2 * wide), f32)] * n
            if column is None
            else [jax.ShapeDtypeStruct((spots, 2 * n * wide), bf16), pltpu.HBM((spots, columns), bf16)]
        )
        + [pltpu.HBM((cells, 2 * wide), bf16)] * n,
        scratch_shapes=[pltpu.VMEM((len(pieces) * rows, 2 * wide), bf16) for pieces in chunks]
        + [pltpu.VMEM((spots, len(used) * rows), bf16)]
        + [pltpu.SemaphoreType.DMA((n, longest))] * 2
        + [pltpu.SemaphoreType.DMA((PIECES,)), pltpu.SemaphoreType.DMA((n, longest))]
        + ([] if column is None else [pltpu.VMEM((spots, 2 * n * wide), bf16), pltpu.SemaphoreType.DMA((1,))]),
        input_output_aliases=aliases,
        compiler_params=params(22),
        cost_estimate=cost(),
        name="forward",
    )(core, in_hbm(mapped), *arrays)
    return results[:outs], results[outs:]


def in_order(core, own, other):
    first = core == 0
    return jnp.concatenate([jnp.where(first, own, other), jnp.where(first, other, own)], axis=1)


def total_of(refs):
    return functools.reduce(jnp.add, [ref[...].astype(f32) for ref in refs])


def stats_kernel(parts, core_ref, *refs):
    own_ref, other_ref, gene_ref, pred_ref, spot_ref = refs[parts:]
    pred = total_of(refs[:parts])
    pred_ref[...] = pred
    target = in_order(core_ref[0], own_ref[...], other_ref[...])
    lane = lax.broadcasted_iota(jnp.int32, spot_ref.shape, 1)
    spot = jnp.zeros(spot_ref.shape, f32)
    for k, term in enumerate((pred * target, pred * pred, target * target)):
        gene_ref[k : k + 1, :] = jnp.sum(term, axis=0, keepdims=True)
        spot = jnp.where(lane == k, jnp.sum(term, axis=1, keepdims=True), spot)
    spot_ref[...] = spot


def pred_stats(core, parts, target, other, column, other_column, wide, part=0):
    spots = parts[0].shape[0]
    whole = pl.BlockSpec((spots, 2 * wide), lambda i, core: (0, 0))
    return pl.pallas_call(
        functools.partial(stats_kernel, len(parts)),
        grid_spec=pltpu.PrefetchScalarGridSpec(
            num_scalar_prefetch=1,
            grid=(1,),
            in_specs=[pl.BlockSpec((spots, 2 * wide), lambda i, core: (0, part))] * len(parts)
            + [
                pl.BlockSpec((spots, wide), lambda i, core: (core[0], column)),
                pl.BlockSpec((spots, wide), lambda i, core: (0, other_column)),
            ],
            out_specs=[
                pl.BlockSpec((3, 2 * wide), lambda i, core: (0, 0)),
                whole,
                pl.BlockSpec((spots, 4), lambda i, core: (0, 0)),
            ],
        ),
        out_shape=[
            jax.ShapeDtypeStruct((3, 2 * wide), f32),
            jax.ShapeDtypeStruct((spots, 2 * wide), f32),
            jax.ShapeDtypeStruct((spots, 4), f32),
        ],
        compiler_params=params(16),
        cost_estimate=cost(),
        name="pred_stats",
    )(core, *parts, target, other)


def grad_pred_kernel(widths, genes_total, spots_total, core_ref, spot_ref, gene_ref, cols_ref, own_ref, *refs):
    n = len(widths)
    other_refs, pred_refs = refs[:3], refs[3 : 3 + n]
    refs = refs[3:]
    quarter = other_refs[0].shape[1]
    turned_ref, col_ref, sums_ref = refs[n:]
    spot = spot_ref[...]
    spot_pg, spot_pp, spot_gg = spot[:, 0:1], spot[:, 1:2], spot[:, 2:3]
    spot_scale = lax.rsqrt(spot_pp + epsilon) * lax.rsqrt(spot_gg + epsilon)
    spot_cos = spot_pg * spot_scale
    spot_back = spot_cos / (spot_pp + epsilon)
    gene = gene_ref[:, : 2 * sum(widths)]
    gene_scale = lax.rsqrt(gene[1:2, :] + epsilon) * lax.rsqrt(gene[2:3, :] + epsilon)
    gene_cos = gene[0:1, :] * gene_scale
    gene_back = gene_cos / (gene[1:2, :] + epsilon)
    gene_pred, gene_target = gene_back / genes_total, gene_scale / genes_total
    spot_pred, spot_target = spot_back / spots_total, spot_scale / spots_total
    folded = jnp.zeros((spot.shape[0], 128), f32)
    at = 0
    low = 0
    for q in range(n):
        wide = widths[q]
        pred = pred_refs[q][...]
        other = other_refs[min(low // quarter, 2)]
        other_low = low - min(low // quarter, 2) * quarter
        target = in_order(core_ref[0], own_ref[:, low : low + wide], other[:, other_low : other_low + wide])
        cols = slice(at, at + 2 * wide)
        grad = pred * (gene_pred[:, cols] + spot_pred) - target * (gene_target[:, cols] + spot_target)
        grad_low = grad.astype(bf16)
        turned_ref[at : at + 2 * wide, :] = grad_low.T
        prod = grad_low.astype(f32) * pred
        for k in range(0, 2 * wide, 128):
            folded = folded + prod[:, k : k + 128]
        at += 2 * wide
        low += wide
    shift, density, counts = cols_ref[0:1, :], cols_ref[1:2, :], cols_ref[2:3, :]
    dens_total = gene_ref[0:1, at : at + 1]
    count_total = gene_ref[2:3, at : at + 1]
    dens_grad = -counts / (count_total * density) + 1.0 / dens_total
    col_ref[0:1, :] = shift
    col_ref[1:2, :] = dens_grad
    col_ref[2:3, :] = jnp.sum(folded.T, axis=0, keepdims=True) + density * dens_grad
    lane = lax.broadcasted_iota(jnp.int32, (1, 128), 1)
    gene_sum = jnp.sum(gene_cos, axis=1, keepdims=True)
    spot_sum = jnp.sum(spot_cos, axis=0, keepdims=True)
    sums_ref[...] = jnp.where(lane == 0, gene_sum, jnp.where(lane == 1, spot_sum, 0.0))


def grad_pred(core, widths, genes_total, spots_total, spot, gene, cols, target, others, preds):
    half = target.shape[1]
    spots = spot.shape[0]
    genes = 2 * half
    return pl.pallas_call(
        functools.partial(grad_pred_kernel, widths, genes_total, spots_total),
        grid_spec=pltpu.PrefetchScalarGridSpec(
            num_scalar_prefetch=1,
            grid=(1,),
            in_specs=[VMEM] * 3
            + [pl.BlockSpec((spots, half), lambda i, core: (core[0], 0))]
            + [VMEM] * (3 + len(preds)),
            out_specs=[VMEM] * 3,
        ),
        out_shape=[
            pltpu.VMEM((genes, spots), bf16),
            jax.ShapeDtypeStruct((3, spots), f32),
            jax.ShapeDtypeStruct((1, 128), f32),
        ],
        compiler_params=params(20),
        cost_estimate=cost(spots * genes * 14, spots * genes * 10),
        name="grad_pred",
    )(core, spot, gene, cols, target, *others, *preds)


def backward_kernel(widths, order_ref, logits_ref, enable_ref, retain_ref, col_ref, turned_ref, *refs):
    n = len(widths)
    panel_refs = refs[:n]
    grad_ref, row_ref = refs[n:]
    rows, spots = logits_ref.shape
    first = pl.multiple_of(pl.program_id(0) * rows, rows)
    enable = enable_ref[...].T
    retain = retain_ref[...].T
    shift, dens, inner = col_ref[0:1, :], col_ref[1:2, :], col_ref[2:3, :]
    part = rows // 2
    for h in range(2):
        here = pl.ds(first + h * part, part)
        near = slice(h * part, (h + 1) * part)
        panel = jnp.concatenate([ref[near if ref.shape[0] == rows else here, :] for ref in panel_refs], axis=1)
        grad_mapped = jnp.dot(panel, turned_ref[...], preferred_element_type=f32) + dens
        for k in range(part // 128):
            at = h * (part // 128) + k
            lines = slice(128 * at, 128 * (at + 1))
            block = jnp.where(enable[:, at : at + 1] > 0, logits_ref[lines, :], -1e30)
            mapping = jnp.exp(block - shift)
            grad = grad_mapped[128 * k : 128 * (k + 1), :]
            grad_ref[lines, :] = mapping * (retain[:, at : at + 1] * grad - inner)
            prod = grad * mapping
            folded = prod[:, 0:128]
            for c in range(128, spots, 128):
                folded = folded + prod[:, c : c + 128]
            row_ref[at : at + 1, :] = jnp.sum(folded.T, axis=0, keepdims=True)


def backward(order, logits, enable, retain, col, turned, panels):
    cells, spots = logits.shape
    genes = turned.shape[0]
    block = cells // PIECES
    widths = tuple(p.shape[1] for p in panels)
    streamed = (0,) + tuple(range(len(panels) - 2, len(panels)))
    cell = pl.BlockSpec((block // 128, 128), lambda i, order: (order[i], 0))
    return pl.pallas_call(
        functools.partial(backward_kernel, widths),
        grid_spec=pltpu.PrefetchScalarGridSpec(
            num_scalar_prefetch=1,
            grid=(PIECES,),
            in_specs=[
                pl.BlockSpec((block, spots), lambda i, order: (order[i], 0)),
                cell,
                cell,
                pl.BlockSpec((3, spots), lambda i, order: (0, 0)),
            ]
            + [VMEM]
            + [pl.BlockSpec((block, w), lambda i, order: (i, 0)) if q in streamed else VMEM for q, w in enumerate(widths)],
            out_specs=[pl.BlockSpec((block, spots), lambda i, order: (order[i], 0)), cell],
        ),
        out_shape=[
            jax.ShapeDtypeStruct((cells, spots), f32),
            jax.ShapeDtypeStruct((cells // 128, 128), f32),
        ],
        compiler_params=params(26),
        cost_estimate=cost(2 * cells * spots * genes, cells * 8 * spots, cells * spots),
        name="backward",
    )(order, logits, enable, retain, col, turned, *[in_hbm(p) if q in streamed else p for q, p in enumerate(panels)])


def final_kernel(genes_total, spots_total, cells_total, copies, sums_ref, gene_ref, count_ref, enable_ref, retain_ref, *refs):
    grad_ref, loss_ref = refs
    n = enable_ref.shape[0]
    last = gene_ref.shape[1] - 1
    offset = (count_ref[...] - 0.5 * cells_total) / cells_total
    penalty = jnp.sqrt(offset * offset + 0.01)
    retain = retain_ref[...]
    retain_grad = sums_ref[0:n, :] + enable_ref[...] * offset / (penalty * cells_total)
    grad_ref[...] = retain_grad * retain * (1.0 - retain)
    dens_total, kl_part, count_total = [gene_ref[k : k + 1, last : last + 1] for k in range(3)]
    kl_term = kl_part / count_total - jnp.log(count_total) + jnp.log(dens_total)
    gene_sum = sums_ref[n : n + 1, 0:1] / copies
    spot_sum = sums_ref[n : n + 1, 1:2]
    loss_ref[...] = -gene_sum / genes_total - spot_sum / spots_total + kl_term + penalty[:, 0:1]


def final(genes_total, spots_total, cells_total, copies, sums, gene, count, enable, retain):
    return pl.pallas_call(
        functools.partial(final_kernel, genes_total, spots_total, cells_total, copies),
        in_specs=[VMEM] * 5,
        out_specs=[VMEM] * 2,
        out_shape=[jax.ShapeDtypeStruct(enable.shape, f32), jax.ShapeDtypeStruct((1, 1), f32)],
        compiler_params=params(12),
        cost_estimate=cost(),
        name="final",
    )(sums, gene, count, enable, retain)


def join_kernel(*refs):
    at = 0
    for ref in refs[:-1]:
        refs[-1][at : at + ref.shape[0], :] = ref[...]
        at += ref.shape[0]


def join(*parts):
    rows = sum(p.shape[0] for p in parts)
    return pl.pallas_call(
        join_kernel,
        in_specs=[VMEM] * len(parts),
        out_specs=VMEM,
        out_shape=jax.ShapeDtypeStruct((rows, parts[0].shape[1]), bf16),
        compiler_params=params(12),
        cost_estimate=cost(0, 4 * rows * parts[0].shape[1]),
        name="join",
    )(*parts)


def select_kernel(inside_ref, b_ref, e_ref, c_ref, f_ref, *out_refs):
    rows = b_ref.shape[0]
    at = 0
    for out in out_refs:
        cols = slice(at, at + out.shape[1])
        at += out.shape[1]
        for flag, refs in ((1, (b_ref, c_ref)), (0, (e_ref, f_ref))):

            @pl.when(inside_ref[0] == flag)
            def _(out=out, refs=refs, cols=cols):
                out[0:rows, :] = refs[0][:, cols]
                out[rows : 2 * rows, :] = refs[1][:, cols]


def select(inside, b, e, c, f, widths):
    rows = b.shape[0]
    return pl.pallas_call(
        select_kernel,
        in_specs=[pl.BlockSpec(memory_space=pltpu.SMEM)] + [VMEM] * 4,
        out_specs=[VMEM] * len(widths),
        out_shape=[jax.ShapeDtypeStruct((2 * rows, wide), bf16) for wide in widths],
        compiler_params=params(12),
        cost_estimate=cost(),
        name="select",
    )(inside, b, e, c, f)


def share_kernel(places, core_ref, *refs):
    kept_ref, sent_ref = refs[-2:]
    first = core_ref[0] == 0
    n = len(places)
    at = 0
    for ref, place in zip(refs, places):
        pred = ref[...]
        wide = pred.shape[1] // 2
        if place is not None:
            left = [x[:, place : place + 2 * wide].astype(f32) for x in refs[n : n + 2]]
            pred = pred + (left[0] + left[1])
        kept_ref[:, at : at + wide] = jnp.where(first, pred[:, :wide], pred[:, wide:])
        sent_ref[:, at : at + wide] = jnp.where(first, pred[:, wide:], pred[:, :wide])
        at += wide


def share(core, preds, left, places):
    spots = preds[0].shape[0]
    wide = sum(p.shape[1] // 2 for p in preds)
    arrays = [*preds, *left]
    return pl.pallas_call(
        functools.partial(share_kernel, places),
        in_specs=[pl.BlockSpec(memory_space=pltpu.SMEM)] + [pl.BlockSpec()] * len(arrays),
        out_specs=[VMEM] * 2,
        out_shape=[jax.ShapeDtypeStruct((spots, wide), f32)] * 2,
        compiler_params=params(24),
        cost_estimate=cost(),
        name="share",
    )(core, *[in_hbm(x) for x in arrays])


def lay_kernel(core_ref, kept_ref, theirs_ref, *refs):
    mine = pl.program_id(0) == core_ref[0]

    @pl.when(mine)
    def _():
        refs[-1][...] = kept_ref[...]

    @pl.when(jnp.logical_not(mine))
    def _():
        refs[-1][...] = theirs_ref[...]


def lay(core, kept, theirs, half, column, begun=None):
    spots, wide = kept.shape
    part = pl.BlockSpec((spots, wide), lambda i, core: (0, 0))
    return pl.pallas_call(
        lay_kernel,
        grid_spec=pltpu.PrefetchScalarGridSpec(
            num_scalar_prefetch=1,
            grid=(2,),
            in_specs=[part, part] + ([] if begun is None else [pl.BlockSpec(memory_space=pl.ANY)]),
            out_specs=pl.BlockSpec((spots, wide), lambda i, core: (i, column)),
        ),
        out_shape=jax.ShapeDtypeStruct((2 * spots, half), f32),
        input_output_aliases={} if begun is None else {3: 0},
        compiler_params=params(16),
        cost_estimate=cost(),
        name="lay",
    )(core, kept, theirs, *(() if begun is None else (begun,)))


def swap_cells(x):
    return lax.ppermute(x, "cells", [(0, 1), (1, 0)])


def swap_genes(x):
    return lax.ppermute(x, "genes", [(0, 1), (1, 0)])


def sum_spots_genes(x, first=(), second=lambda *_: ()):
    if lax.axis_size("spots") != 8:
        return lax.psum(x, ("spots", "genes")), second(*first)
    moved = [lax.ppermute(x, "spots", [(i, i ^ d) for i in range(8)]) for d in (2, 4, 6)]
    moved[0], moved[1], moved[2], *first = hold(*moved, *first)
    x = (x + moved[0]) + (moved[1] + moved[2])
    pairs = [lax.ppermute(x, ("spots", "genes"), [(i, i ^ d) for i in range(16)]) for d in (1, 2, 3)]
    pairs[0], pairs[1], pairs[2], *more = hold(*pairs, *second(*first))
    return (x + pairs[0]) + (pairs[1] + pairs[2]), more


class Step:
    def __init__(self, logits, filter_logits, expression, spot_expression, cell_mask, spot_counts):
        self.logits = pltpu.with_memory_space_constraint(logits, pltpu.HBM)
        self.expression = expression
        self.core = lax.axis_index("genes")
        self.enable = cell_mask.astype(f32).reshape(-1, 128)
        self.retain = jax.nn.sigmoid(filter_logits).reshape(-1, 128)
        self.spots = logits.shape[1]
        self.counts = spot_counts.astype(f32)[None, :]
        self.core_flag = self.core.astype(jnp.int32).reshape(1)
        self.half = expression.shape[1]
        self.target = spot_expression
        sent = lax.dynamic_slice_in_dim(spot_expression, (1 - self.core) * self.spots, self.spots, 0)
        quarter = self.half // 4
        self.target_sent = [sent[:, :quarter], sent[:, quarter : 2 * quarter], sent[:, 2 * quarter :]]

    def local_stats(self):
        part = col_stats(self.logits, self.enable, self.retain)
        count = jnp.broadcast_to(jnp.sum(self.enable * self.retain), (1, self.spots))
        return jnp.concatenate([part, count], axis=0)

    def merge_stats(self, part, away):
        top = jnp.maximum(part[0], away[0])
        here, there = jnp.exp(part[0] - top), jnp.exp(away[0] - top)
        total = part[1] * here + away[1] * there
        density = (part[2] * here + away[2] * there) / total
        self.density = density[None, :]
        self.cell_count = part[3:4, :128] + away[3:4, :128]
        self.shift = (top + jnp.log(total))[None, :]
        counts = self.counts[0]
        kl_parts = (jnp.sum(density), jnp.sum(counts * (jnp.log(counts) - jnp.log(density))), jnp.sum(counts))
        self.kl_parts = jnp.broadcast_to(jnp.stack(kl_parts)[:, None], (3, 128))

    def turned(self, order, shift, logits):
        return mapped_turned(order, logits, self.enable, self.retain, shift)

    def stats(self, parts, other, at, wide, part=0):
        begin = self.half - other.shape[1] if other.shape[1] > self.half // 4 else at // (self.half // 4) * (self.half // 4)
        return pred_stats(self.core_flag, parts, self.target, other, at // wide, (at - begin) // wide, wide, part)

    def gathered_whole(self):
        own = lax.all_gather(self.expression, "spots", axis=0, tiled=True)
        other = swap_genes(own)
        part = self.local_stats()
        self.target_other = [swap_genes(x) for x in self.target_sent]
        self.merge_stats(part, swap_cells(part))
        order = jnp.arange(PIECES, dtype=jnp.int32)
        mapped = self.turned(order, self.shift, self.logits)
        wide = self.half // 4
        widths, panels, stats = (wide,) * 4, [], []
        for q in range(4):
            pieces = tuple((r, 0, r, q) for r in range(PIECES))
            (partial,), (panel,) = forward(self.core_flag, mapped, [(own, other)], [pieces], wide)
            panels.append(panel)
            stats.append(self.stats([lax.psum(partial, "cells")], self.target_other[min(q, 2)], q * wide, wide))
        return order, widths, panels, stats, (), None

    def gathered_line(self):
        near_pairs = [(2 * z + y, 2 * (z ^ 1) + y) for z in range(4) for y in range(2)]
        middle_pairs = [(2 * z + y, 2 * (3 - z) + y) for z in (1, 2) for y in range(2)]
        across_pairs = [(i, i ^ 1) for i in range(8)]

        def near(x):
            return lax.ppermute(x, "spots", near_pairs)

        def middle(x):
            return lax.ppermute(x, "spots", middle_pairs)

        def across(x):
            return lax.ppermute(x, "spots", across_pairs)

        spot = lax.axis_index("spots")
        z, y = spot // 2, spot % 2
        inside = (z == 1) | (z == 2)
        inside_flag = inside.astype(jnp.int32).reshape(1)
        column = jnp.stack([z, z ^ 1, jnp.where(z < 2, 2, 1), jnp.where(z < 2, 3, 0)])
        order = jnp.concatenate([2 * column + y, 2 * column + (1 - y)]).astype(jnp.int32)
        unit = self.half // 8
        expr = self.expression

        def cut(x, at, wide):
            return x[:, at * unit : (at + wide) * unit]

        def pick(b, e, c, f, *widths):
            return select(inside_flag, b, e, c, f, [wide * unit for wide in widths])

        core = self.core_flag

        def run(sources, chunks, wide, begun=None, near=False, column=None, columns=0, left=None):
            columns = (None if column is None else 2 * column * unit), 2 * columns * unit
            return forward(core, mapped, sources, chunks, wide * unit, begun, near, *columns, left)

        def whole(c, d):
            return ((0, 0, 0, c), (1, 1, 0, d), (2, 2, 0, 0), (3, 2, 1, 0), (4, 3, 0, c), (5, 4, 0, d), (6, 5, 0, 0), (7, 5, 1, 0))

        s01 = cut(expr, 0, 4)
        beside = across(expr)
        a01 = near(s01)
        b01 = middle(s01)
        expr_o = swap_genes(expr)
        target_0 = swap_genes(self.target_sent[0])
        part = self.local_stats()
        a01, b01, part, target_0, sv, target_1 = hold(
            a01, b01, part, target_0, cut(expr, 4, 3), self.target_sent[1]
        )
        c01 = middle(a01)
        e01 = near(b01)
        away = swap_cells(part)
        target_1 = swap_genes(target_1)
        self.merge_stats(part, away)
        mapped = self.turned(order, self.shift, self.logits)
        beside, e01, c01, expr_o, mapped, a01, sv, target_1 = hold(
            beside, e01, c01, expr_o, mapped, a01, sv, target_1
        )
        yn = across(a01)
        f01 = near(c01)
        beside_o = swap_genes(beside)
        a01_o = swap_genes(a01)
        bv = middle(sv)
        yn, f01, a01_o, sv, bv, beside, self.kl_parts = hold(yn, f01, a01_o, sv, bv, beside, self.kl_parts)
        mf0, mf1 = pick(b01, e01, c01, f01, 2, 2)
        ymf0 = across(mf0)
        av = near(sv)
        mf0_o, yn_o = swap_genes(mf0), swap_genes(yn)
        sf = join(cut(expr, 7, 1), cut(beside, 7, 1))
        expr_2, a01_2, beside_2, yn_2 = (expr, expr_o), (a01, a01_o), (beside, beside_o), (yn, yn_o)
        begun = run([expr_2, beside_2], [((0, 0, 0, q), (4, 1, 0, q)) for q in range(4, 8)], 1)
        ymf0, av, mf0_o, yn_o, mf1, bv, mapped, *begun = hold(
            ymf0, av, mf0_o, yn_o, mf1, bv, mapped, *begun[0], *begun[1]
        )
        ymf1 = across(mf1)
        ev = near(bv)
        cv = middle(av)
        ymf0_o, mf1_o = swap_genes(ymf0), swap_genes(mf1)
        (high0, low0), (panel0,) = run(
            [expr_2, a01_2, (mf0, mf0_o), beside_2, yn_2, (ymf0, ymf0_o)], [whole(0, 0)], 2, column=0, columns=2
        )
        ymf1, ev, cv, high0, mf1_o, av, mapped = hold(ymf1, ev, cv, high0, mf1_o, av, mapped)
        ynv = across(av)
        fv = near(cv)
        ymf1_o = swap_genes(ymf1)
        high0_away = swap_cells(high0)
        av_o = swap_genes(av)
        (partial1,), (panel1,) = run([expr_2, a01_2, (mf1, mf1_o), beside_2, yn_2, (ymf1, ymf1_o)], [whole(1, 1)], 2)
        ynv, fv, partial1, high0_away, av_o, sf, mapped = hold(ynv, fv, partial1, high0_away, av_o, sf, mapped)
        m2, m34 = pick(bv, ev, cv, fv, 1, 2)
        ym2 = across(m2)
        af, bf = near(sf), middle(sf)
        away1 = swap_cells(partial1)
        ynv_o = swap_genes(ynv)
        more = run(
            [(av, av_o), (ynv, ynv_o)], [((1, 0, 0, q), (5, 1, 0, q)) for q in range(3)], 1, (begun[0:3], begun[4:7])
        )
        ym2, af, bf, m2, m34, mapped, *more = hold(ym2, af, bf, m2, m34, mapped, *more[0], *more[1])
        ym34 = across(m34)
        cf = middle(af)
        ym2_o, m2_o = swap_genes(ym2), swap_genes(m2)

        def rest(column):
            return ((2, 0, 0, column), (3, 0, 1, column), (6, 1, 0, column), (7, 1, 1, column))

        (high2, low), (panel2,) = run(
            [(m2, m2_o), (ym2, ym2_o)], [rest(0)], 1, (more[0:1], more[3:4]), near=True, column=0, columns=4
        )
        stats0 = self.stats([high0, high0_away], target_0, 0, 2 * unit)
        cf, high2, away1, m34, bf, af, *stats0 = hold(cf, high2, away1, m34, bf, af, *stats0)
        ef, ff = near(bf), near(cf)
        m34_o = swap_genes(m34)
        high2_away = swap_cells(high2)
        stats1 = self.stats([partial1, away1], target_1, 2 * unit, 2 * unit)
        ym34, ef, m34, mapped, high2_away, af, low0, *stats1 = hold(
            ym34, ef, m34, mapped, high2_away, af, low0, *stats1
        )
        ym34_o, af_o = swap_genes(ym34), swap_genes(af)
        low0_away = swap_cells(low0)
        (high34, low), (panel3, panel4) = run(
            [(m34, m34_o), (ym34, ym34_o)],
            [rest(0), rest(1)],
            1,
            (more[1:3], more[4:6]),
            near=True,
            column=1,
            columns=4,
            left=low,
        )
        ff, high34, af_o, low0_away, mapped = hold(ff, high34, af_o, low0_away, mapped)
        high34_away = swap_cells(high34)
        (mff,) = pick(bf, ef, cf, ff, 1)
        mff_o = swap_genes(mff)
        late = ((1, 0, 0, 0), (2, 1, 0, 0), (3, 1, 2, 0), (5, 0, 1, 0), (6, 1, 1, 0), (7, 1, 3, 0))
        (highf, low), (panelf,) = run(
            [(af, af_o), (mff, mff_o)], [late], 1, (begun[3:4], begun[7:8]), column=3, columns=4, left=low
        )
        highf, high34_away, target_2 = hold(highf, high34_away, self.target_sent[2])
        highf_away = swap_cells(highf)
        target_2 = swap_genes(target_2)
        self.target_other = (target_0, target_1, target_2)
        late = [
            self.stats([high2, high2_away], target_2, 4 * unit, unit),
            self.stats([high34, high34_away], target_2, 5 * unit, unit),
            self.stats([high34, high34_away], target_2, 6 * unit, unit, 1),
            self.stats([highf, highf_away], target_2, 7 * unit, unit),
        ]
        widths = (2 * unit,) * 2 + (unit,) * 4
        panels = (panel0, panel1, panel2, panel3, panel4, panelf)
        return order, widths, panels, [stats0, stats1, *late], (low0, low0_away), low


def body(logits, filter_logits, expression, spot_expression, cell_mask, spot_counts):
    cells_total = logits.shape[0] * lax.axis_size("cells")
    spots = logits.shape[1]
    spots_total = spots * lax.axis_size("spots") * lax.axis_size("genes")
    genes_total = expression.shape[1] * lax.axis_size("genes")
    step = Step(logits, filter_logits, expression, spot_expression, cell_mask, spot_counts)
    gathered = step.gathered_line() if lax.axis_size("spots") == 8 else step.gathered_whole()
    order, widths, panels, stats, left, late_left = gathered
    gene_stats, preds, spot_stats = zip(*stats)
    split = 2
    gene, (kept, sent) = sum_spots_genes(
        jnp.concatenate([*gene_stats, step.kl_parts], axis=1),
        preds[:split],
        lambda *first: share(step.core_flag, first, left, [0, None] if left else [None] * split),
    )
    spot = functools.reduce(jnp.add, spot_stats)
    cols = jnp.concatenate([step.shift, step.density, step.counts], axis=0)
    turned, col, sums = grad_pred(
        step.core_flag, widths, genes_total, spots_total, spot, gene, cols, step.target, step.target_other, preds
    )
    left, places = [], [None] * (len(widths) - split)
    if late_left is not None:
        turned, late_left = hold(turned, late_left)
        left, places = [late_left, swap_cells(late_left)], [2 * sum(widths[split:q]) for q in range(split, len(widths))]
    turned, sent = hold(turned, sent)
    theirs = swap_genes(sent)
    grad_logits, row = backward(order, step.logits, step.enable, step.retain, col, turned, panels)

    row, core, theirs, *left = hold(row, step.core_flag, theirs, *left)
    half = expression.shape[1]

    def lay_both(late_kept, late_sent):
        predicted = lay(core, kept, theirs, half, 0)
        return (lay(core, late_kept, swap_genes(late_sent), half, 1, predicted),)

    row_sums, (predicted,) = sum_spots_genes(jnp.concatenate([row, sums], axis=0), share(core, preds[split:], left, places), lay_both)
    copies = lax.axis_size("spots") * lax.axis_size("genes")
    filter_grad, total_loss = final(
        genes_total, spots_total, cells_total, copies, row_sums, gene, step.cell_count, step.enable, step.retain
    )
    return (predicted, total_loss.reshape(()), grad_logits, filter_grad.reshape(-1))


def solution(mesh):
    placed = (
        P("cells", ("spots", "genes")),
        P("cells"),
        P(("cells", "spots"), "genes"),
        P("spots", "genes"),
        P("cells"),
        P(("spots", "genes")),
    )
    return jax.shard_map(
        body,
        mesh=mesh,
        in_specs=placed,
        out_specs=(P("spots", "genes"), P(), P("cells", ("spots", "genes")), P("cells")),
        check_vma=False,
    )
```

profile of v0, /device:TPU:0, one launch (start us, length us, event | category | flops | bytes accessed | tf_op | source)
XLA Modules:
  0.0 299.8 jit_solution(6346906620794956168)
XLA Ops:
  2.9 3.0 %collective-permute-start = (bf16[1024,512]{1,0:T(8,128)(2,1)}, bf16[1024,512]{1,0:T(8,128)(2,1)}, u32[]{:S(2)}, u32[]{:S(2)}) collective-permute-start(bf16[1024,512]{1,0:T(8,128)(2,1)} %slice.47), channel_id=1, source_target_pairs={{0,4},{2,6},{4,0},{6,2},{8,12},{10,14},{12,8},{14,10},{1,5},{3,7},... | collective-permute-start | bytes 3145736 | tf_op jit(solution)/shard_map/ppermute | solution.py:646
  10.7 10.9 %col_stats.1 = f32[3,512]{1,0:T(4,128)S(1)} custom-call(f32[8192,512]{1,0:T(8,128)} %logits_ref.5, f32[64,128]{1,0:T(8,128)S(1)} %convert_bitcast_fusion.enable_ref, f32[64,128]{1,0:T(8,128)S(1)} %get-tuple-element.370.retain_ref), custom_call_target="tpu_custom_call" | custom-call | flops 1 | bytes 1 | tf_op jit(solution)/shard_map/col_stats/pallas_call | solution.py:76
  24.4 5.0 %collective-permute-done.refs_1_ = bf16[1024,512]{1,0:T(8,128)(2,1)} collective-permute-done((bf16[1024,512]{1,0:T(8,128)(2,1)}, bf16[1024,512]{1,0:T(8,128)(2,1)}, u32[]{:S(2)}, u32[]{:S(2)}) %collective-permute-start) | collective-permute-done | bytes 1048608 | tf_op jit(solution)/shard_map/ppermute | solution.py:646
  29.4 4.7 %collective-permute-start.4 = (bf16[1024,512]{1,0:T(8,128)(2,1)S(1)}, bf16[1024,512]{1,0:T(8,128)(2,1)}, u32[]{:S(2)}, u32[]{:S(2)}) collective-permute-start(bf16[1024,512]{1,0:T(8,128)(2,1)S(1)} %collective-permute-done.1.b_ref), channel_id=1, source_target_pairs={{0,4},{2,6},{4,0},{6,2},{8,12},{10,14},{12,8},{14,10},{1,5},{3,7},... | collective-permute-start | bytes 3145736 | tf_op jit(solution)/shard_map/ppermute | solution.py:646
  39.6 15.6 %mapped_turned.1.mapped_ref = bf16[512,8192]{1,0:T(8,128)(2,1)} custom-call(s32[8]{0:T(128)S(1)} %pad_add_fusion.order_ref, f32[8192,512]{1,0:T(8,128)} %logits_ref.5, f32[64,128]{1,0:T(8,128)S(1)} %convert_bitcast_fusion.enable_ref, f32[64,128]{1,0:T(8,128)S(1)} %get-tuple-element.370.retain_ref, f32[1,512]{1,0:T(1,128)S(1)} %get-tuple-element.372.shift_ref), custom_call_target="tpu_custom_call" | custom-call | flops 1 | bytes 1 | tf_op jit(solution)/shard_map/mapped_turned/pallas_call | solution.py:104
  58.1 3.8 %collective-permute-start.10 = (bf16[1024,512]{1,0:T(8,128)(2,1)}, bf16[1024,512]{1,0:T(8,128)(2,1)}, u32[]{:S(2)}, u32[]{:S(2)}) collective-permute-start(bf16[1024,512]{1,0:T(8,128)(2,1)} %collective-permute-done.5.c_ref), channel_id=1, source_target_pairs={{0,4},{2,6},{4,0},{6,2},{8,12},{10,14},{12,8},{14,10},{1,5},{3,7},... | collective-permute-start | bytes 3145736 | tf_op jit(solution)/shard_map/ppermute | solution.py:646
  66.7 14.5 %collective-permute-done.9.refs_4_ = bf16[1024,512]{1,0:T(8,128)(2,1)} collective-permute-done((bf16[1024,512]{1,0:T(8,128)(2,1)}, bf16[1024,512]{1,0:T(8,128)(2,1)}, u32[]{:S(2)}, u32[]{:S(2)}) %collective-permute-start.9) | collective-permute-done | bytes 1048608 | tf_op jit(solution)/shard_map/ppermute | solution.py:652
  88.4 8.4 %forward.7 = (f32[512,256]{1,0:T(8,128)S(1)}, f32[512,256]{1,0:T(8,128)S(1)}, f32[512,256]{1,0:T(8,128)S(1)}, f32[512,256]{1,0:T(8,128)S(1)}, bf16[8192,256]{1,0...) custom-call(s32[1]{0:T(128)} %bitcast.6.core_ref, ...), custom_call_target="tpu_custom_call" | custom-call | flops 1 | bytes 1 | tf_op jit(solution)/shard_map/forward/pallas_call | solution.py:218
  96.8 9.5 %collective-permute-done.14.refs_0_ = bf16[1024,384]{1,0:T(8,128)(2,1)S(1)} collective-permute-done((bf16[1024,384]{1,0:T(8,128)(2,1)}, bf16[1024,384]{1,0:T(8,128)(2,1)S(1)}, u32[]{:S(2)}, u32[]{:S(2)}) %collective-permute-start.14) | collective-permute-done | bytes 786464 | tf_op jit(solution)/shard_map/ppermute | solution.py:646
  108.7 2.6 collective-permute-start.19
  113.2 9.9 %forward.8 = (bf16[512,512]{1,0:T(8,128)(2,1)S(1)}, bf16[512,512]{1,0:T(8,128)(2,1)}, bf16[8192,512]{1,0:T(8,128)(2,1)}) custom-call(s32[1]{0:T(128)} %bitcast.6.core_ref, bf16[512,8192]{1,0:T(8,128)(2,1)} %mapped_turned.1.mapped_ref, bf16[1024,1024]{1,0:T(8,128)(2,1)} %refs_0_.5, bf16[1024,512]{1,0:T(8,128)(2,1)} %collective-permute-done.refs_1_, ...), custom_call_target="tpu_custom_call" | custom-call | flops 1 | bytes 1 | tf_op jit(solution)/shard_map/forward/pallas_call | solution.py:218
  123.2 6.4 %collective-permute-done.19.e_ref = bf16[1024,384]{1,0:T(8,128)(2,1)S(1)} collective-permute-done((bf16[1024,384]{1,0:T(8,128)(2,1)}, bf16[1024,384]{1,0:T(8,128)(2,1)S(1)}, u32[]{:S(2)}, u32[]{:S(2)}) %collective-permute-start.19) | collective-permute-done | bytes 786464 | tf_op jit(solution)/shard_map/ppermute | solution.py:646
  129.6 4.0 %collective-permute-done.18.refs_5_ = bf16[2048,256]{1,0:T(8,128)(2,1)S(1)} collective-permute-done((bf16[2048,256]{1,0:T(8,128)(2,1)S(1)}, bf16[2048,256]{1,0:T(8,128)(2,1)S(1)}, u32[]{:S(2)}, u32[]{:S(2)}) %collective-permute-start.18) | collective-permute-done | bytes 1048608 | tf_op jit(solution)/shard_map/ppermute | solution.py:652
  134.2 2.6 collective-permute-start.24
  141.3 9.5 %forward.9 = (f32[512,512]{1,0:T(8,128)S(1)}, bf16[8192,512]{1,0:T(8,128)(2,1)}) custom-call(s32[1]{0:T(128)} %bitcast.6.core_ref, bf16[512,8192]{1,0:T(8,128)(2,1)} %mapped_turned.1.mapped_ref, bf16[1024,1024]{1,0:T(8,128)(2,1)} %refs_0_.5, bf16[1024,512]{1,0:T(8,128)(2,1)} %collective-permute-done.refs_1_, bf16[2048,256]{1,0:T(8,128)(2,1)} %copy-done.17, ...), custom_call_target="tpu_custom_call" | custom-call | flops 1 | bytes 1 | tf_op jit(solution)/shard_map/forward/pallas_call | solution.py:218
  151.2 2.4 collective-permute-done.23.refs_1_
  162.8 6.6 %forward.10 = (f32[512,256]{1,0:T(8,128)S(1)}, f32[512,256]{1,0:T(8,128)S(1)}, f32[512,256]{1,0:T(8,128)S(1)}, bf16[8192,256]{1,0:T(8,128)(2,1)}, bf16[8192,256]{1,0:T(8,128)(2,1)}, /*index=5*/bf16[8192,256]{1,0:T(8,128)(2,1)}) custom-call(s32[1]{0:T(128)} %bitcast.6.core_ref, ...), custom_call_target="tpu_custom_call", output_to_operand_aliasing={{3}: (9, {}), {4}: (10, {}), {5}: (11, {})} | custom-call | flops 1 | bytes 1 | tf_op jit(solution)/shard_map/forward/pallas_call | solution.py:218
  175.0 4.8 %forward.11 = (bf16[512,256]{1,0:T(8,128)(2,1)S(1)}, bf16[512,1024]{1,0:T(8,128)(2,1)}, bf16[8192,256]{1,0:T(8,128)(2,1)}) custom-call(s32[1]{0:T(128)} %bitcast.6.core_ref, bf16[512,8192]{1,0:T(8,128)(2,1)} %mapped_turned.1.mapped_ref, bf16[2048,128]{1,0:T(8,128)(2,1)S(1)} %get-tuple-element.246.refs_0_, ...), custom_call_target="tpu_custom_call", output_to_operand_aliasing={{2}: (7, {})} | custom-call | flops 1 | bytes 1 | tf_op jit(solution)/shard_map/forward/pallas_call | solution.py:218
  179.9 5.3 %collective-permute-done.35.refs_1_ = f32[512,512]{1,0:T(8,128)S(1)} collective-permute-done((f32[512,512]{1,0:T(8,128)S(1)}, f32[512,512]{1,0:T(8,128)S(1)}, u32[]{:S(2)}, u32[]{:S(2)}) %collective-permute-start.35) | collective-permute-done | bytes 1048608 | tf_op jit(solution)/shard_map/ppermute | solution.py:565
  185.1 6.4 %collective-permute-start.37 = (bf16[2048,128]{1,0:T(8,128)(2,1)S(1)}, bf16[2048,128]{1,0:T(8,128)(2,1)S(1)}, u32[]{:S(2)}, u32[]{:S(2)}) collective-permute-start(bf16[2048,128]{1,0:T(8,128)(2,1)S(1)} %collective-permute-done.30.b_ref), channel_id=1, source_target_pairs={{0,4},{2,6},{4,0},{6,2},{8,12},{10,14},{12,8},{14,10},{1,5},{3,7},... | collective-permute-start | bytes 1572872 | tf_op jit(solution)/shard_map/ppermute | solution.py:646
  194.6 4.0 %collective-permute-done.38.refs_1_ = bf16[512,256]{1,0:T(8,128)(2,1)S(1)} collective-permute-done((bf16[512,256]{1,0:T(8,128)(2,1)S(1)}, bf16[512,256]{1,0:T(8,128)(2,1)S(1)}, u32[]{:S(2)}, u32[]{:S(2)}) %collective-permute-start.38) | collective-permute-done | bytes 262176 | tf_op jit(solution)/shard_map/ppermute | solution.py:565
  198.6 4.1 %collective-permute-done.37.e_ref = bf16[2048,128]{1,0:T(8,128)(2,1)S(1)} collective-permute-done((bf16[2048,128]{1,0:T(8,128)(2,1)S(1)}, bf16[2048,128]{1,0:T(8,128)(2,1)S(1)}, u32[]{:S(2)}, u32[]{:S(2)}) %collective-permute-start.37) | collective-permute-done | bytes 524320 | tf_op jit(solution)/shard_map/ppermute | solution.py:646
  206.2 7.5 %forward.12 = (bf16[512,512]{1,0:T(8,128)(2,1)S(1)}, bf16[512,1024]{1,0:T(8,128)(2,1)}, bf16[8192,256]{1,0:T(8,128)(2,1)}, bf16[8192,256]{1,0:T(8,128)(2,1)}) custom-call(s32[1]{0:T(128)} %bitcast.6.core_ref, bf16[512,8192]{1,0:T(8,128)(2,1)} %mapped_turned.1.mapped_ref, ...), custom_call_target="tpu_custom_call", output_to_operand_aliasing={{2}: (8, {}), {3}: (9, {}), {1}: (10, {})} | custom-call | flops 1 | bytes 1 | tf_op jit(solution)/shard_map/forward/pallas_call | solution.py:218
  213.8 3.3 %collective-permute-done.39.f_ref = bf16[2048,128]{1,0:T(8,128)(2,1)S(1)} collective-permute-done((bf16[2048,128]{1,0:T(8,128)(2,1)S(1)}, bf16[2048,128]{1,0:T(8,128)(2,1)S(1)}, u32[]{:S(2)}, u32[]{:S(2)}) %collective-permute-start.39) | collective-permute-done | bytes 524320 | tf_op jit(solution)/shard_map/ppermute | solution.py:646
  222.5 6.9 %forward.13 = (bf16[512,256]{1,0:T(8,128)(2,1)S(1)}, bf16[512,1024]{1,0:T(8,128)(2,1)}, bf16[8192,256]{1,0:T(8,128)(2,1)}) custom-call(s32[1]{0:T(128)} %bitcast.6.core_ref, bf16[512,8192]{1,0:T(8,128)(2,1)} %mapped_turned.1.mapped_ref, bf16[2048,128]{1,0:T(8,128)(2,1)} %copy-done.38, ...), custom_call_target="tpu_custom_call", output_to_operand_aliasing={{2}: (7, {}), {1}: (8, {})} | custom-call | flops 1 | bytes 1 | tf_op jit(solution)/shard_map/forward/pallas_call | solution.py:218
  229.4 4.3 %collective-permute-done.45.refs_1_ = bf16[512,512]{1,0:T(8,128)(2,1)S(1)} collective-permute-done((bf16[512,512]{1,0:T(8,128)(2,1)S(1)}, bf16[512,512]{1,0:T(8,128)(2,1)S(1)}, u32[]{:S(2)}, u32[]{:S(2)}) %collective-permute-start.45) | collective-permute-done | bytes 524320 | tf_op jit(solution)/shard_map/ppermute | solution.py:565
  237.6 4.9 %collective-permute-done.47.refs_1_ = bf16[512,256]{1,0:T(8,128)(2,1)S(1)} collective-permute-done((bf16[512,256]{1,0:T(8,128)(2,1)S(1)}, bf16[512,256]{1,0:T(8,128)(2,1)S(1)}, u32[]{:S(2)}, u32[]{:S(2)}) %collective-permute-start.47) | collective-permute-done | bytes 262176 | tf_op jit(solution)/shard_map/ppermute | solution.py:565
  243.3 2.5 collective-permute-start.49
  248.4 3.1 %collective-permute-done.50 = f32[3,2176]{1,0:T(4,128)S(1)} collective-permute-done((f32[3,2176]{1,0:T(4,128)S(1)}, f32[3,2176]{1,0:T(4,128)S(1)}, u32[]{:S(2)}, u32[]{:S(2)}) %collective-permute-start.50) | collective-permute-done | bytes 26144 | tf_op jit(solution)/shard_map/ppermute | solution.py:575
  260.1 25.8 %backward.1 = (f32[8192,512]{1,0:T(8,128)}, f32[64,128]{1,0:T(8,128)S(1)}) custom-call(s32[8]{0:T(128)S(1)} %pad_add_fusion.order_ref, f32[8192,512]{1,0:T(8,128)} %logits_ref.5, f32[64,128]{1,0:T(8,128)S(1)} %convert_bitcast_fusion.enable_ref, f32[64,128]{1,0:T(8,128)S(1)} %get-tuple-element.370.retain_ref, f32[3,512]{1,0:T(4,128)S(1)} %get-tuple-element.324.col_ref, ...), custom_call_target="tpu_custom_call" | custom-call | flops 1 | bytes 1 | tf_op jit(solution)/shard_map/backward/pallas_call | solution.py:402
  288.1 2.3 collective-permute-start.58
  290.4 2.7 share.3
  (249 shorter events, 91.0 us)
Async XLA Ops:
  2.9 26.5 %collective-permute-start = (bf16[1024,512]{1,0:T(8,128)(2,1)}, bf16[1024,512]{1,0:T(8,128)(2,1)}, u32[]{:S(2)}, u32[]{:S(2)}) collective-permute-start(bf16[1024,512]{1,0:T(8,128)(2,1)} %slice.47), channel_id=1, source_target_pairs={{0,4},{2,6},{4,0},{6,2},{8,12},{10,14},{12,8},{14,10},{1,5},{3,7},... | collective-permute-start | bytes 3145736 | tf_op jit(solution)/shard_map/ppermute | solution.py:646
  5.9 23.5 %collective-permute-start.1 = (bf16[1024,512]{1,0:T(8,128)(2,1)}, bf16[1024,512]{1,0:T(8,128)(2,1)S(1)}, u32[]{:S(2)}, u32[]{:S(2)}) collective-permute-start(bf16[1024,512]{1,0:T(8,128)(2,1)} %slice.47), channel_id=1, source_target_pairs={{4,8},{6,10},{8,4},{10,6},{5,9},{7,11},{9,5},{11,7},{20,24},{22,26... | collective-permute-start | bytes 3145736 | tf_op jit(solution)/shard_map/ppermute | solution.py:649
  6.7 48.6 %collective-permute-start.3 = (bf16[1024,1024]{1,0:T(8,128)(2,1)}, bf16[1024,1024]{1,0:T(8,128)(2,1)}, u32[]{:S(2)}, u32[]{:S(2)}) collective-permute-start(bf16[1024,1024]{1,0:T(8,128)(2,1)} %refs_0_.5), channel_id=1, source_target_pairs={{0,2},{2,0},{4,6},{6,4},{8,10},{10,8},{12,14},{14,12},{1,3},{3,1},... | collective-permute-start | bytes 6291464 | tf_op jit(solution)/shard_map/ppermute | solution.py:652
  8.3 48.3 %collective-permute-start.6 = (bf16[1024,1024]{1,0:T(8,128)(2,1)}, bf16[1024,1024]{1,0:T(8,128)(2,1)}, u32[]{:S(2)}, u32[]{:S(2)}) collective-permute-start(bf16[1024,1024]{1,0:T(8,128)(2,1)} %refs_0_.5), channel_id=1, source_target_pairs={{0,1},{1,0},{2,3},{3,2},{4,5},{5,4},{6,7},{7,6},{8,9},{9,8},{10,11... | collective-permute-start | bytes 6291464 | tf_op jit(solution)/shard_map/ppermute | solution.py:569
  9.5 14.8 %collective-permute-start.2 = (f32[512,256]{1,0:T(8,128)S(1)}, f32[512,256]{1,0:T(8,128)S(1)}, u32[]{:S(2)}, u32[]{:S(2)}) collective-permute-start(f32[512,256]{1,0:T(8,128)S(1)} %get-tuple-element.368), channel_id=1, source_target_pairs={{0,1},{1,0},{2,3},{3,2},{4,5},{5,4},{6,7},{7,6},{8,9},{9,8},{10,11... | collective-permute-start | bytes 1572872 | tf_op jit(solution)/shard_map/ppermute | solution.py:569
  29.4 27.2 %collective-permute-start.4 = (bf16[1024,512]{1,0:T(8,128)(2,1)S(1)}, bf16[1024,512]{1,0:T(8,128)(2,1)}, u32[]{:S(2)}, u32[]{:S(2)}) collective-permute-start(bf16[1024,512]{1,0:T(8,128)(2,1)S(1)} %collective-permute-done.1.b_ref), channel_id=1, source_target_pairs={{0,4},{2,6},{4,0},{6,2},{8,12},{10,14},{12,8},{14,10},{1,5},{3,7},... | collective-permute-start | bytes 3145736 | tf_op jit(solution)/shard_map/ppermute | solution.py:646
  34.1 22.5 %collective-permute-start.5 = (bf16[1024,512]{1,0:T(8,128)(2,1)}, bf16[1024,512]{1,0:T(8,128)(2,1)}, u32[]{:S(2)}, u32[]{:S(2)}) collective-permute-start(bf16[1024,512]{1,0:T(8,128)(2,1)} %collective-permute-done.refs_1_), channel_id=1, source_target_pairs={{4,8},{6,10},{8,4},{10,6},{5,9},{7,11},{9,5},{11,7},{20,24},{22,26... | collective-permute-start | bytes 3145736 | tf_op jit(solution)/shard_map/ppermute | solution.py:649
  39.4 15.8 %collective-permute-start.8 = (f32[512,256]{1,0:T(8,128)S(1)}, f32[512,256]{1,0:T(8,128)S(1)}, u32[]{:S(2)}, u32[]{:S(2)}) collective-permute-start(f32[512,256]{1,0:T(8,128)S(1)} %get-tuple-element.186), channel_id=1, source_target_pairs={{0,1},{1,0},{2,3},{3,2},{4,5},{5,4},{6,7},{7,6},{8,9},{9,8},{10,11... | collective-permute-start | bytes 1572872 | tf_op jit(solution)/shard_map/ppermute | solution.py:569
  56.6 24.6 %collective-permute-start.9 = (bf16[1024,512]{1,0:T(8,128)(2,1)}, bf16[1024,512]{1,0:T(8,128)(2,1)}, u32[]{:S(2)}, u32[]{:S(2)}) collective-permute-start(bf16[1024,512]{1,0:T(8,128)(2,1)} %collective-permute-done.refs_1_), channel_id=1, source_target_pairs={{0,2},{2,0},{4,6},{6,4},{8,10},{10,8},{12,14},{14,12},{1,3},{3,1},... | collective-permute-start | bytes 3145736 | tf_op jit(solution)/shard_map/ppermute | solution.py:652
  58.1 25.3 %collective-permute-start.10 = (bf16[1024,512]{1,0:T(8,128)(2,1)}, bf16[1024,512]{1,0:T(8,128)(2,1)}, u32[]{:S(2)}, u32[]{:S(2)}) collective-permute-start(bf16[1024,512]{1,0:T(8,128)(2,1)} %collective-permute-done.5.c_ref), channel_id=1, source_target_pairs={{0,4},{2,6},{4,0},{6,2},{8,12},{10,14},{12,8},{14,10},{1,5},{3,7},... | collective-permute-start | bytes 3145736 | tf_op jit(solution)/shard_map/ppermute | solution.py:646
  61.9 21.5 %collective-permute-start.11 = (bf16[1024,512]{1,0:T(8,128)(2,1)}, bf16[1024,512]{1,0:T(8,128)(2,1)}, u32[]{:S(2)}, u32[]{:S(2)}) collective-permute-start(bf16[1024,512]{1,0:T(8,128)(2,1)} %collective-permute-done.refs_1_), channel_id=1, source_target_pairs={{0,1},{1,0},{2,3},{3,2},{4,5},{5,4},{6,7},{7,6},{8,9},{9,8},{10,11... | collective-permute-start | bytes 3145736 | tf_op jit(solution)/shard_map/ppermute | solution.py:569
  61.9 26.4 %collective-permute-start.17 = (bf16[1024,1024]{1,0:T(8,128)(2,1)}, bf16[1024,1024]{1,0:T(8,128)(2,1)}, u32[]{:S(2)}, u32[]{:S(2)}) collective-permute-start(bf16[1024,1024]{1,0:T(8,128)(2,1)} %collective-permute-done.3.refs_1_.refs_3_), channel_id=1, source_target_pairs={{0,1},{1,0},{2,3},{3,2},{4,5},{5,4},{6,7},{7,6},{8,9},{9,8},{10,11... | collective-permute-start | bytes 6291464 | tf_op jit(solution)/shard_map/ppermute | solution.py:569
  85.5 22.4 %collective-permute-start.13 = (bf16[2048,256]{1,0:T(8,128)(2,1)S(1)}, bf16[2048,256]{1,0:T(8,128)(2,1)S(1)}, u32[]{:S(2)}, u32[]{:S(2)}) collective-permute-start(bf16[2048,256]{1,0:T(8,128)(2,1)S(1)} %get-tuple-element.193.refs_2_), channel_id=1, source_target_pairs={{0,2},{2,0},{4,6},{6,4},{8,10},{10,8},{12,14},{14,12},{1,3},{3,1},... | collective-permute-start | bytes 3145736 | tf_op jit(solution)/shard_map/ppermute | solution.py:652
  86.1 21.8 %collective-permute-start.15 = (bf16[2048,256]{1,0:T(8,128)(2,1)S(1)}, bf16[2048,256]{1,0:T(8,128)(2,1)S(1)}, u32[]{:S(2)}, u32[]{:S(2)}) collective-permute-start(bf16[2048,256]{1,0:T(8,128)(2,1)S(1)} %get-tuple-element.193.refs_2_), channel_id=1, source_target_pairs={{0,1},{1,0},{2,3},{3,2},{4,5},{5,4},{6,7},{7,6},{8,9},{9,8},{10,11... | collective-permute-start | bytes 3145736 | tf_op jit(solution)/shard_map/ppermute | solution.py:569
  86.1 21.8 %collective-permute-start.16 = (bf16[1024,512]{1,0:T(8,128)(2,1)}, bf16[1024,512]{1,0:T(8,128)(2,1)S(1)}, u32[]{:S(2)}, u32[]{:S(2)}) collective-permute-start(bf16[1024,512]{1,0:T(8,128)(2,1)} %collective-permute-done.9.refs_4_), channel_id=1, source_target_pairs={{0,1},{1,0},{2,3},{3,2},{4,5},{5,4},{6,7},{7,6},{8,9},{9,8},{10,11... | collective-permute-start | bytes 3145736 | tf_op jit(solution)/shard_map/ppermute | solution.py:569
  86.6 19.7 %collective-permute-start.14 = (bf16[1024,384]{1,0:T(8,128)(2,1)}, bf16[1024,384]{1,0:T(8,128)(2,1)S(1)}, u32[]{:S(2)}, u32[]{:S(2)}) collective-permute-start(bf16[1024,384]{1,0:T(8,128)(2,1)} %slice.49), channel_id=1, source_target_pairs={{0,4},{2,6},{4,0},{6,2},{8,12},{10,14},{12,8},{14,10},{1,5},{3,7},... | collective-permute-start | bytes 2359304 | tf_op jit(solution)/shard_map/ppermute | solution.py:646
  108.0 25.6 %collective-permute-start.18 = (bf16[2048,256]{1,0:T(8,128)(2,1)S(1)}, bf16[2048,256]{1,0:T(8,128)(2,1)S(1)}, u32[]{:S(2)}, u32[]{:S(2)}) collective-permute-start(bf16[2048,256]{1,0:T(8,128)(2,1)S(1)} %get-tuple-element.210.refs_2_), channel_id=1, source_target_pairs={{0,2},{2,0},{4,6},{6,4},{8,10},{10,8},{12,14},{14,12},{1,3},{3,1},... | collective-permute-start | bytes 3145736 | tf_op jit(solution)/shard_map/ppermute | solution.py:652
  108.6 25.0 %collective-permute-start.22 = (bf16[2048,256]{1,0:T(8,128)(2,1)S(1)}, bf16[2048,256]{1,0:T(8,128)(2,1)S(1)}, u32[]{:S(2)}, u32[]{:S(2)}) collective-permute-start(bf16[2048,256]{1,0:T(8,128)(2,1)S(1)} %get-tuple-element.210.refs_2_), channel_id=1, source_target_pairs={{0,1},{1,0},{2,3},{3,2},{4,5},{5,4},{6,7},{7,6},{8,9},{9,8},{10,11... | collective-permute-start | bytes 3145736 | tf_op jit(solution)/shard_map/ppermute | solution.py:569
  108.7 20.9 %collective-permute-start.19 = (bf16[1024,384]{1,0:T(8,128)(2,1)}, bf16[1024,384]{1,0:T(8,128)(2,1)S(1)}, u32[]{:S(2)}, u32[]{:S(2)}) collective-permute-start(bf16[1024,384]{1,0:T(8,128)(2,1)} %collective-permute-done.12.b_ref), channel_id=1, source_target_pairs={{0,4},{2,6},{4,0},{6,2},{8,12},{10,14},{12,8},{14,10},{1,5},{3,7},... | collective-permute-start | bytes 2359304 | tf_op jit(solution)/shard_map/ppermute | solution.py:646
  111.3 18.3 %collective-permute-start.20 = (bf16[1024,384]{1,0:T(8,128)(2,1)S(1)}, bf16[1024,384]{1,0:T(8,128)(2,1)S(1)}, u32[]{:S(2)}, u32[]{:S(2)}) collective-permute-start(bf16[1024,384]{1,0:T(8,128)(2,1)S(1)} %collective-permute-done.14.refs_0_), channel_id=1, source_target_pairs={{4,8},{6,10},{8,4},{10,6},{5,9},{7,11},{9,5},{11,7},{20,24},{22,26... | collective-permute-start | bytes 2359304 | tf_op jit(solution)/shard_map/ppermute | solution.py:649
  133.7 20.0 %collective-permute-start.23 = (bf16[1024,384]{1,0:T(8,128)(2,1)S(1)}, bf16[1024,384]{1,0:T(8,128)(2,1)S(1)}, u32[]{:S(2)}, u32[]{:S(2)}) collective-permute-start(bf16[1024,384]{1,0:T(8,128)(2,1)S(1)} %collective-permute-done.14.refs_0_), channel_id=1, source_target_pairs={{0,2},{2,0},{4,6},{6,4},{8,10},{10,8},{12,14},{14,12},{1,3},{3,1},... | collective-permute-start | bytes 2359304 | tf_op jit(solution)/shard_map/ppermute | solution.py:652
  134.2 20.5 %collective-permute-start.24 = (bf16[1024,384]{1,0:T(8,128)(2,1)S(1)}, bf16[1024,384]{1,0:T(8,128)(2,1)S(1)}, u32[]{:S(2)}, u32[]{:S(2)}) collective-permute-start(bf16[1024,384]{1,0:T(8,128)(2,1)S(1)} %collective-permute-done.20.c_ref), channel_id=1, source_target_pairs={{0,4},{2,6},{4,0},{6,2},{8,12},{10,14},{12,8},{14,10},{1,5},{3,7},... | collective-permute-start | bytes 2359304 | tf_op jit(solution)/shard_map/ppermute | solution.py:646
  136.8 17.9 %collective-permute-start.27 = (bf16[1024,384]{1,0:T(8,128)(2,1)S(1)}, bf16[1024,384]{1,0:T(8,128)(2,1)S(1)}, u32[]{:S(2)}, u32[]{:S(2)}) collective-permute-start(bf16[1024,384]{1,0:T(8,128)(2,1)S(1)} %collective-permute-done.14.refs_0_), channel_id=1, source_target_pairs={{0,1},{1,0},{2,3},{3,2},{4,5},{5,4},{6,7},{7,6},{8,9},{9,8},{10,11... | collective-permute-start | bytes 2359304 | tf_op jit(solution)/shard_map/ppermute | solution.py:569
  136.8 14.3 %collective-permute-start.26 = (bf16[512,512]{1,0:T(8,128)(2,1)S(1)}, bf16[512,512]{1,0:T(8,128)(2,1)S(1)}, u32[]{:S(2)}, u32[]{:S(2)}) collective-permute-start(bf16[512,512]{1,0:T(8,128)(2,1)S(1)} %get-tuple-element.224.refs_0_), channel_id=1, source_target_pairs={{0,16},{16,0},{1,17},{17,1},{2,18},{18,2},{3,19},{19,3},{4,20},{20... | collective-permute-start | bytes 1572872 | tf_op jit(solution)/shard_map/ppermute | solution.py:565
  156.3 14.1 %collective-permute-start.28 = (bf16[2048,128]{1,0:T(8,128)(2,1)S(1)}, bf16[2048,128]{1,0:T(8,128)(2,1)S(1)}, u32[]{:S(2)}, u32[]{:S(2)}) collective-permute-start(bf16[2048,128]{1,0:T(8,128)(2,1)S(1)} %get-tuple-element.246.refs_0_), channel_id=1, source_target_pairs={{0,2},{2,0},{4,6},{6,4},{8,10},{10,8},{12,14},{14,12},{1,3},{3,1},... | collective-permute-start | bytes 1572872 | tf_op jit(solution)/shard_map/ppermute | solution.py:652
  160.3 24.8 %collective-permute-start.35 = (f32[512,512]{1,0:T(8,128)S(1)}, f32[512,512]{1,0:T(8,128)S(1)}, u32[]{:S(2)}, u32[]{:S(2)}) collective-permute-start(f32[512,512]{1,0:T(8,128)S(1)} %get-tuple-element.251.refs_0_), channel_id=1, source_target_pairs={{0,16},{16,0},{1,17},{17,1},{2,18},{18,2},{3,19},{19,3},{4,20},{20... | collective-permute-start | bytes 3145736 | tf_op jit(solution)/shard_map/ppermute | solution.py:565
  172.9 25.7 %collective-permute-start.36 = (bf16[2048,256]{1,0:T(8,128)(2,1)S(1)}, bf16[2048,256]{1,0:T(8,128)(2,1)S(1)}, u32[]{:S(2)}, u32[]{:S(2)}) collective-permute-start(bf16[2048,256]{1,0:T(8,128)(2,1)S(1)} %get-tuple-element.274.refs_0_), channel_id=1, source_target_pairs={{0,2},{2,0},{4,6},{6,4},{8,10},{10,8},{12,14},{14,12},{1,3},{3,1},... | collective-permute-start | bytes 3145736 | tf_op jit(solution)/shard_map/ppermute | solution.py:652
  185.1 17.6 %collective-permute-start.37 = (bf16[2048,128]{1,0:T(8,128)(2,1)S(1)}, bf16[2048,128]{1,0:T(8,128)(2,1)S(1)}, u32[]{:S(2)}, u32[]{:S(2)}) collective-permute-start(bf16[2048,128]{1,0:T(8,128)(2,1)S(1)} %collective-permute-done.30.b_ref), channel_id=1, source_target_pairs={{0,4},{2,6},{4,0},{6,2},{8,12},{10,14},{12,8},{14,10},{1,5},{3,7},... | collective-permute-start | bytes 1572872 | tf_op jit(solution)/shard_map/ppermute | solution.py:646
  202.8 14.3 %collective-permute-start.39 = (bf16[2048,128]{1,0:T(8,128)(2,1)S(1)}, bf16[2048,128]{1,0:T(8,128)(2,1)S(1)}, u32[]{:S(2)}, u32[]{:S(2)}) collective-permute-start(bf16[2048,128]{1,0:T(8,128)(2,1)S(1)} %collective-permute-done.32.c_ref), channel_id=1, source_target_pairs={{0,4},{2,6},{4,0},{6,2},{8,12},{10,14},{12,8},{14,10},{1,5},{3,7},... | collective-permute-start | bytes 1572872 | tf_op jit(solution)/shard_map/ppermute | solution.py:646
  204.7 14.1 %collective-permute-start.43 = (bf16[512,512]{1,0:T(8,128)(2,1)S(1)}, bf16[512,512]{1,0:T(8,128)(2,1)S(1)}, u32[]{:S(2)}, u32[]{:S(2)}) collective-permute-start(bf16[512,512]{1,0:T(8,128)(2,1)S(1)} %copy-done.40), channel_id=1, source_target_pairs={{0,16},{16,0},{1,17},{17,1},{2,18},{18,2},{3,19},{19,3},{4,20},{20... | collective-permute-start | bytes 1572872 | tf_op jit(solution)/shard_map/ppermute | solution.py:565
  258.4 27.5 %collective-permute-start.54 = (f32[512,512]{1,0:T(8,128)S(1)}, f32[512,512]{1,0:T(8,128)S(1)}, u32[]{:S(2)}, u32[]{:S(2)}) collective-permute-start(f32[512,512]{1,0:T(8,128)S(1)} %get-tuple-element.337), channel_id=1, source_target_pairs={{0,1},{1,0},{2,3},{3,2},{4,5},{5,4},{6,7},{7,6},{8,9},{9,8},{10,11... | collective-permute-start | bytes 3145736 | tf_op jit(solution)/shard_map/ppermute | solution.py:569
  258.6 27.3 %collective-permute-start.55 = (bf16[512,1024]{1,0:T(8,128)(2,1)S(1)}, bf16[512,1024]{1,0:T(8,128)(2,1)S(1)}, u32[]{:S(2)}, u32[]{:S(2)}) collective-permute-start(bf16[512,1024]{1,0:T(8,128)(2,1)S(1)} %copy-done.25), channel_id=1, source_target_pairs={{0,16},{16,0},{1,17},{17,1},{2,18},{18,2},{3,19},{19,3},{4,20},{20... | collective-permute-start | bytes 3145736 | tf_op jit(solution)/shard_map/ppermute | solution.py:565
  (78 other events, 902.2 us)
where the time goes:
time: 301 us; the launch traced here: 300 us
  Pallas kernels  123 us (41%)
  waiting for transfers between devices  87.4 us (29%)
  starting transfers between devices  69.3 us (23%)
  local copies, waits for them, and re-layouts  15 us (5%)
  other arithmetic  3.71 us (1%)
    pallas_call x7, Pallas kernels, forward(): pl.pallas_call(functools.partial(forward_kernel, chunks, len(own), rows,...  53.6 us
    ppermute x9, waiting for transfers between devices, near(): return lax.ppermute(x, 'spots', near_pairs)  34.3 us
    ppermute x9, starting transfers between devices, near(): return lax.ppermute(x, 'spots', near_pairs)  28.4 us
    pallas_call x1, Pallas kernels, backward(): pl.pallas_call(functools.partial(backward_kernel, widths), grid_spec=pltp...  25.8 us
    ppermute x7, waiting for transfers between devices, across(): return lax.ppermute(x, 'spots', across_pairs)  23.5 us
    ppermute x8, waiting for transfers between devices, swap_cells(): return lax.ppermute(x, 'cells', [(0, 1), (1, 0)])  22.7 us
    pallas_call x1, Pallas kernels, mapped_turned(): pl.pallas_call(mapped_kernel, grid_spec=pltpu.PrefetchScalarGridSpec(num_...  15.6 us
    ppermute x8, starting transfers between devices, swap_cells(): return lax.ppermute(x, 'cells', [(0, 1), (1, 0)])  12.1 us
  transfers between devices with their start and end apart: 63, of which 27 were waited for; matrix products, arithmetic and copies ran while one was open for 4% of the time, Pallas kernels for 40%

commit v1 on v0

--- a/solution.py
+++ b/solution.py
@@ -484,15 +484,17 @@
             def _(out=out, refs=refs, cols=cols):
                 out[0:rows, :] = refs[0][:, cols]
                 out[rows : 2 * rows, :] = refs[1][:, cols]
-
-
-def select(inside, b, e, c, f, widths):
+                if out.shape[0] > 2 * rows:
+                    out[2 * rows :, :] = jnp.zeros_like(out[2 * rows :, :])
+
+
+def select(inside, b, e, c, f, widths, pad):
     rows = b.shape[0]
     return pl.pallas_call(
         select_kernel,
         in_specs=[pl.BlockSpec(memory_space=pltpu.SMEM)] + [VMEM] * 4,
         out_specs=[VMEM] * len(widths),
-        out_shape=[jax.ShapeDtypeStruct((2 * rows, wide), bf16) for wide in widths],
+        out_shape=[jax.ShapeDtypeStruct((2 * rows + pad * k, wide), bf16) for k, wide in enumerate(widths)],
         compiler_params=params(12),
         cost_estimate=cost(),
         name="select",
@@ -663,8 +665,8 @@
         def cut(x, at, wide):
             return x[:, at * unit : (at + wide) * unit]
 
-        def pick(b, e, c, f, *widths):
-            return select(inside_flag, b, e, c, f, [wide * unit for wide in widths])
+        def pick(b, e, c, f, *widths, pad=0):
+            return select(inside_flag, b, e, c, f, [wide * unit for wide in widths], pad)
 
         core = self.core_flag
 
@@ -699,8 +701,10 @@
         beside_o = swap_genes(beside)
         a01_o = swap_genes(a01)
         bv = middle(sv)
-        yn, f01, a01_o, sv, bv, beside, self.kl_parts = hold(yn, f01, a01_o, sv, bv, beside, self.kl_parts)
         mf0, mf1 = pick(b01, e01, c01, f01, 2, 2)
+        yn, mf0, mf1, a01_o, sv, bv, beside, self.kl_parts = hold(
+            yn, mf0, mf1, a01_o, sv, bv, beside, self.kl_parts
+        )
         ymf0 = across(mf0)
         av = near(sv)
         mf0_o, yn_o = swap_genes(mf0), swap_genes(yn)
@@ -725,7 +729,7 @@
         av_o = swap_genes(av)
         (partial1,), (panel1,) = run([expr_2, a01_2, (mf1, mf1_o), beside_2, yn_2, (ymf1, ymf1_o)], [whole(1, 1)], 2)
         ynv, fv, partial1, high0_away, av_o, sf, mapped = hold(ynv, fv, partial1, high0_away, av_o, sf, mapped)
-        m2, m34 = pick(bv, ev, cv, fv, 1, 2)
+        m2, m34 = pick(bv, ev, cv, fv, 1, 2, pad=16)
         ym2 = across(m2)
         af, bf = near(sf), middle(sf)
         away1 = swap_cells(partial1)
@@ -733,10 +737,11 @@
         more = run(
             [(av, av_o), (ynv, ynv_o)], [((1, 0, 0, q), (5, 1, 0, q)) for q in range(3)], 1, (begun[0:3], begun[4:7])
         )
-        ym2, af, bf, m2, m34, mapped, *more = hold(ym2, af, bf, m2, m34, mapped, *more[0], *more[1])
+        ym2, m2, m34, mapped, *more = hold(ym2, m2, m34, mapped, *more[0], *more[1])
         ym34 = across(m34)
+        ym2_o, m2_o = swap_genes(ym2), swap_genes(m2)
+        af, bf = hold(af, bf)
         cf = middle(af)
-        ym2_o, m2_o = swap_genes(ym2), swap_genes(m2)
 
         def rest(column):
             return ((2, 0, 0, column), (3, 0, 1, column), (6, 1, 0, column), (7, 1, 1, column))
@@ -750,22 +755,23 @@
         m34_o = swap_genes(m34)
         high2_away = swap_cells(high2)
         stats1 = self.stats([partial1, away1], target_1, 2 * unit, 2 * unit)
-        ym34, ef, m34, mapped, high2_away, af, low0, *stats1 = hold(
-            ym34, ef, m34, mapped, high2_away, af, low0, *stats1
+        ym34, ef, m34, mapped, high2_away, af, low0, target_2, *stats1 = hold(
+            ym34, ef, m34, mapped, high2_away, af, low0, self.target_sent[2], *stats1
         )
         ym34_o, af_o = swap_genes(ym34), swap_genes(af)
         low0_away = swap_cells(low0)
+        target_2 = swap_genes(target_2)
+        self.target_other = (target_0, target_1, target_2)
         (high34, low), (panel3, panel4) = run(
             [(m34, m34_o), (ym34, ym34_o)],
             [rest(0), rest(1)],
             1,
             (more[1:3], more[4:6]),
-            near=True,
             column=1,
             columns=4,
             left=low,
         )
-        ff, high34, af_o, low0_away, mapped = hold(ff, high34, af_o, low0_away, mapped)
+        ff, high34, low0_away, target_2, af_o, mapped = hold(ff, high34, low0_away, target_2, af_o, mapped)
         high34_away = swap_cells(high34)
         (mff,) = pick(bf, ef, cf, ff, 1)
         mff_o = swap_genes(mff)
@@ -773,10 +779,9 @@
         (highf, low), (panelf,) = run(
             [(af, af_o), (mff, mff_o)], [late], 1, (begun[3:4], begun[7:8]), column=3, columns=4, left=low
         )
-        highf, high34_away, target_2 = hold(highf, high34_away, self.target_sent[2])
+        highf, high2, high2_away = hold(highf, high2, high2_away)
         highf_away = swap_cells(highf)
-        target_2 = swap_genes(target_2)
-        self.target_other = (target_0, target_1, target_2)
+        high34, high34_away, highf = hold(high34, high34_away, highf)
         late = [
             self.stats([high2, high2_away], target_2, 4 * unit, unit),
             self.stats([high34, high34_away], target_2, 5 * unit, unit),

time: 301 us -> 295 us (0.980)
  waiting for transfers between devices: 87.4 us -> 71.8 us
  local copies, waits for them, and re-layouts: 15 us -> 23.1 us
    ppermute x7, waiting for transfers between devices: 23.5 us -> 8.57 us  [across(): return lax.ppermute(x, 'spots', across_pairs)]
    unnamed x101 -> x115, local copies, waits for them, and re-layouts: 5.39 us -> 13.5 us
    ppermute x8, waiting for transfers between devices: 22.7 us -> 16 us  [swap_cells(): return lax.ppermute(x, 'cells', [(0, 1), (1, 0)])]
    ppermute x9, waiting for transfers between devices: 34.3 us -> 39.3 us  [near(): return lax.ppermute(x, 'spots', near_pairs)]
    ppermute x9, starting transfers between devices: 28.4 us -> 24.4 us  [near(): return lax.ppermute(x, 'spots', near_pairs)]
  transfers between devices with their start and end apart: 63 -> 63, of which waited for: 27 -> 25; matrix products, arithmetic and copies ran while one was open for 4% -> 4% of each run, Pallas kernels for 40% -> 41%
where the time goes in v1:
time: 295 us; the launch traced here: 294 us
  Pallas kernels  125 us (42%)
  waiting for transfers between devices  71.8 us (24%)
  starting transfers between devices  68.4 us (23%)
  local copies, waits for them, and re-layouts  23.1 us (8%)
  other arithmetic  3.54 us (1%)
    pallas_call x7, Pallas kernels, forward(): pl.pallas_call(functools.partial(forward_kernel, chunks, len(own), rows,...  54.5 us
    ppermute x9, waiting for transfers between devices, near(): return lax.ppermute(x, 'spots', near_pairs)  39.3 us
    pallas_call x1, Pallas kernels, backward(): pl.pallas_call(functools.partial(backward_kernel, widths), grid_spec=pltp...  25.6 us
    ppermute x9, starting transfers between devices, near(): return lax.ppermute(x, 'spots', near_pairs)  24.4 us
    ppermute x8, waiting for transfers between devices, swap_cells(): return lax.ppermute(x, 'cells', [(0, 1), (1, 0)])  16 us
    pallas_call x1, Pallas kernels, mapped_turned(): pl.pallas_call(mapped_kernel, grid_spec=pltpu.PrefetchScalarGridSpec(num_...  15.6 us
    unnamed x115, local copies, waits for them, and re-layouts  13.5 us
    ppermute x8, starting transfers between devices, swap_cells(): return lax.ppermute(x, 'cells', [(0, 1), (1, 0)])  12.1 us
  transfers between devices with their start and end apart: 63, of which 25 were waited for; matrix products, arithmetic and copies ran while one was open for 4% of the time, Pallas kernels for 41%

profile of v1, /device:TPU:0, one launch (start us, length us, event | category | flops | bytes accessed | tf_op | source)
XLA Modules:
  0.0 293.8 jit_solution(3475888605857372424)
XLA Ops:
  2.0 3.1 %collective-permute-start.1 = (bf16[1024,512]{1,0:T(8,128)(2,1)S(1)}, bf16[1024,512]{1,0:T(8,128)(2,1)}, u32[]{:S(2)}, u32[]{:S(2)}) collective-permute-start(bf16[1024,512]{1,0:T(8,128)(2,1)S(1)} %slice.47), channel_id=1, source_target_pairs={{0,4},{2,6},{4,0},{6,2},{8,12},{10,14},{12,8},{14,10},{1,5},{3,7},... | collective-permute-start | bytes 3145736 | tf_op jit(solution)/shard_map/ppermute | solution.py:648
  7.4 2.1 fusion.4
  10.6 10.9 %col_stats.1 = f32[3,512]{1,0:T(4,128)S(1)} custom-call(f32[8192,512]{1,0:T(8,128)} %logits_ref.5, f32[64,128]{1,0:T(8,128)S(1)} %convert_bitcast_fusion.enable_ref, f32[64,128]{1,0:T(8,128)S(1)} %get-tuple-element.382.retain_ref), custom_call_target="tpu_custom_call" | custom-call | flops 1 | bytes 1 | tf_op jit(solution)/shard_map/col_stats/pallas_call | solution.py:76
  21.4 2.1 slice.49
  24.2 4.1 %collective-permute-done.1.refs_1_ = bf16[1024,512]{1,0:T(8,128)(2,1)} collective-permute-done((bf16[1024,512]{1,0:T(8,128)(2,1)S(1)}, bf16[1024,512]{1,0:T(8,128)(2,1)}, u32[]{:S(2)}, u32[]{:S(2)}) %collective-permute-start.1) | collective-permute-done | bytes 1048608 | tf_op jit(solution)/shard_map/ppermute | solution.py:648
  28.3 4.7 %collective-permute-start.4 = (bf16[1024,512]{1,0:T(8,128)(2,1)S(1)}, bf16[1024,512]{1,0:T(8,128)(2,1)S(1)}, u32[]{:S(2)}, u32[]{:S(2)}) collective-permute-start(bf16[1024,512]{1,0:T(8,128)(2,1)S(1)} %collective-permute-done.2.b_ref), channel_id=1, source_target_pairs={{0,4},{2,6},{4,0},{6,2},{8,12},{10,14},{12,8},{14,10},{1,5},{3,7},... | collective-permute-start | bytes 3145736 | tf_op jit(solution)/shard_map/ppermute | solution.py:648
  36.2 2.2 collective-permute-done.7
  38.5 15.6 %mapped_turned.1.mapped_ref = bf16[512,8192]{1,0:T(8,128)(2,1)} custom-call(s32[8]{0:T(128)S(1)} %pad_add_fusion.order_ref, f32[8192,512]{1,0:T(8,128)} %logits_ref.5, f32[64,128]{1,0:T(8,128)S(1)} %convert_bitcast_fusion.enable_ref, f32[64,128]{1,0:T(8,128)S(1)} %get-tuple-element.382.retain_ref, f32[1,512]{1,0:T(1,128)S(1)} %get-tuple-element.384.shift_ref), custom_call_target="tpu_custom_call" | custom-call | flops 1 | bytes 1 | tf_op jit(solution)/shard_map/mapped_turned/pallas_call | solution.py:104
  55.4 3.9 %collective-permute-start.10 = (bf16[1024,512]{1,0:T(8,128)(2,1)}, bf16[1024,512]{1,0:T(8,128)(2,1)}, u32[]{:S(2)}, u32[]{:S(2)}) collective-permute-start(bf16[1024,512]{1,0:T(8,128)(2,1)} %collective-permute-done.5.c_ref), channel_id=1, source_target_pairs={{0,4},{2,6},{4,0},{6,2},{8,12},{10,14},{12,8},{14,10},{1,5},{3,7},... | collective-permute-start | bytes 3145736 | tf_op jit(solution)/shard_map/ppermute | solution.py:648
  65.5 15.6 %collective-permute-done.10.f_ref = bf16[1024,512]{1,0:T(8,128)(2,1)} collective-permute-done((bf16[1024,512]{1,0:T(8,128)(2,1)}, bf16[1024,512]{1,0:T(8,128)(2,1)}, u32[]{:S(2)}, u32[]{:S(2)}) %collective-permute-start.10) | collective-permute-done | bytes 1048608 | tf_op jit(solution)/shard_map/ppermute | solution.py:648
  86.7 8.4 %forward.7 = (f32[512,256]{1,0:T(8,128)S(1)}, f32[512,256]{1,0:T(8,128)S(1)}, f32[512,256]{1,0:T(8,128)S(1)}, f32[512,256]{1,0:T(8,128)S(1)}, bf16[8192,256]{1,0...) custom-call(s32[1]{0:T(128)} %bitcast.6.core_ref, ...), custom_call_target="tpu_custom_call" | custom-call | flops 1 | bytes 1 | tf_op jit(solution)/shard_map/forward/pallas_call | solution.py:218
  95.9 8.7 %collective-permute-done.14.refs_0_ = bf16[1024,384]{1,0:T(8,128)(2,1)S(1)} collective-permute-done((bf16[1024,384]{1,0:T(8,128)(2,1)}, bf16[1024,384]{1,0:T(8,128)(2,1)S(1)}, u32[]{:S(2)}, u32[]{:S(2)}) %collective-permute-start.14) | collective-permute-done | bytes 786464 | tf_op jit(solution)/shard_map/ppermute | solution.py:648
  110.7 9.9 %forward.8 = (bf16[512,512]{1,0:T(8,128)(2,1)S(1)}, bf16[512,512]{1,0:T(8,128)(2,1)}, bf16[8192,512]{1,0:T(8,128)(2,1)}) custom-call(s32[1]{0:T(128)} %bitcast.6.core_ref, bf16[512,8192]{1,0:T(8,128)(2,1)} %mapped_turned.1.mapped_ref, bf16[1024,1024]{1,0:T(8,128)(2,1)} %refs_0_.5, bf16[1024,512]{1,0:T(8,128)(2,1)} %collective-permute-done.1.refs_1_, ...), custom_call_target="tpu_custom_call" | custom-call | flops 1 | bytes 1 | tf_op jit(solution)/shard_map/forward/pallas_call | solution.py:218
  120.7 6.7 %collective-permute-done.19.e_ref = bf16[1024,384]{1,0:T(8,128)(2,1)S(1)} collective-permute-done((bf16[1024,384]{1,0:T(8,128)(2,1)}, bf16[1024,384]{1,0:T(8,128)(2,1)S(1)}, u32[]{:S(2)}, u32[]{:S(2)}) %collective-permute-start.19) | collective-permute-done | bytes 786464 | tf_op jit(solution)/shard_map/ppermute | solution.py:648
  127.3 3.8 %collective-permute-done.18.refs_5_ = bf16[2048,256]{1,0:T(8,128)(2,1)S(1)} collective-permute-done((bf16[2048,256]{1,0:T(8,128)(2,1)S(1)}, bf16[2048,256]{1,0:T(8,128)(2,1)S(1)}, u32[]{:S(2)}, u32[]{:S(2)}) %collective-permute-start.18) | collective-permute-done | bytes 1048608 | tf_op jit(solution)/shard_map/ppermute | solution.py:654
  138.8 9.5 %forward.9 = (f32[512,512]{1,0:T(8,128)S(1)}, bf16[8192,512]{1,0:T(8,128)(2,1)}) custom-call(s32[1]{0:T(128)} %bitcast.6.core_ref, bf16[512,8192]{1,0:T(8,128)(2,1)} %mapped_turned.1.mapped_ref, bf16[1024,1024]{1,0:T(8,128)(2,1)} %refs_0_.5, bf16[1024,512]{1,0:T(8,128)(2,1)} %collective-permute-done.1.refs_1_, bf16[2048,256]{1,0:T(8,128)(2,1)} %copy-done.15, ...), custom_call_target="tpu_custom_call" | custom-call | flops 1 | bytes 1 | tf_op jit(solution)/shard_map/forward/pallas_call | solution.py:218
  148.6 2.6 collective-permute-done.23.refs_1_
  160.3 6.5 %forward.10 = (f32[512,256]{1,0:T(8,128)S(1)}, f32[512,256]{1,0:T(8,128)S(1)}, f32[512,256]{1,0:T(8,128)S(1)}, bf16[8192,256]{1,0:T(8,128)(2,1)}, bf16[8192,256]{1,0:T(8,128)(2,1)}, /*index=5*/bf16[8192,256]{1,0:T(8,128)(2,1)}) custom-call(s32[1]{0:T(128)} %bitcast.6.core_ref, ...), custom_call_target="tpu_custom_call", output_to_operand_aliasing={{3}: (9, {}), {4}: (10, {}), {5}: (11, {})} | custom-call | flops 1 | bytes 1 | tf_op jit(solution)/shard_map/forward/pallas_call | solution.py:218
  171.5 4.8 %forward.11 = (bf16[512,256]{1,0:T(8,128)(2,1)S(1)}, bf16[512,1024]{1,0:T(8,128)(2,1)}, bf16[8192,256]{1,0:T(8,128)(2,1)}) custom-call(s32[1]{0:T(128)} %bitcast.6.core_ref, bf16[512,8192]{1,0:T(8,128)(2,1)} %mapped_turned.1.mapped_ref, bf16[2048,128]{1,0:T(8,128)(2,1)S(1)} %get-tuple-element.253.refs_0_, ...), custom_call_target="tpu_custom_call", output_to_operand_aliasing={{2}: (7, {})} | custom-call | flops 1 | bytes 1 | tf_op jit(solution)/shard_map/forward/pallas_call | solution.py:218
  176.4 6.2 %collective-permute-done.35.refs_1_ = f32[512,512]{1,0:T(8,128)S(1)} collective-permute-done((f32[512,512]{1,0:T(8,128)S(1)}, f32[512,512]{1,0:T(8,128)S(1)}, u32[]{:S(2)}, u32[]{:S(2)}) %collective-permute-start.35) | collective-permute-done | bytes 1048608 | tf_op jit(solution)/shard_map/ppermute | solution.py:567
  183.7 4.5 %collective-permute-start.37 = (bf16[2048,128]{1,0:T(8,128)(2,1)}, bf16[2048,128]{1,0:T(8,128)(2,1)}, u32[]{:S(2)}, u32[]{:S(2)}) collective-permute-start(bf16[2048,128]{1,0:T(8,128)(2,1)} %collective-permute-done.29.b_ref), channel_id=1, source_target_pairs={{0,4},{2,6},{4,0},{6,2},{8,12},{10,14},{12,8},{14,10},{1,5},{3,7},... | collective-permute-start | bytes 1572872 | tf_op jit(solution)/shard_map/ppermute | solution.py:648
  191.2 2.2 copy-done.1
  204.1 8.5 %forward.12 = (bf16[512,512]{1,0:T(8,128)(2,1)S(1)}, bf16[512,1024]{1,0:T(8,128)(2,1)}, bf16[8192,256]{1,0:T(8,128)(2,1)}, bf16[8192,256]{1,0:T(8,128)(2,1)}) custom-call(s32[1]{0:T(128)} %bitcast.6.core_ref, bf16[512,8192]{1,0:T(8,128)(2,1)} %mapped_turned.1.mapped_ref, ...), custom_call_target="tpu_custom_call", output_to_operand_aliasing={{2}: (8, {}), {3}: (9, {}), {1}: (10, {})} | custom-call | flops 1 | bytes 1 | tf_op jit(solution)/shard_map/forward/pallas_call | solution.py:218
  219.9 6.9 %forward.13 = (bf16[512,256]{1,0:T(8,128)(2,1)S(1)}, bf16[512,1024]{1,0:T(8,128)(2,1)}, bf16[8192,256]{1,0:T(8,128)(2,1)}) custom-call(s32[1]{0:T(128)} %bitcast.6.core_ref, bf16[512,8192]{1,0:T(8,128)(2,1)} %mapped_turned.1.mapped_ref, bf16[2048,128]{1,0:T(8,128)(2,1)} %copy-done.44, ...), custom_call_target="tpu_custom_call", output_to_operand_aliasing={{2}: (7, {}), {1}: (8, {})} | custom-call | flops 1 | bytes 1 | tf_op jit(solution)/shard_map/forward/pallas_call | solution.py:218
  231.8 4.4 %collective-permute-done.47.refs_1_ = bf16[512,256]{1,0:T(8,128)(2,1)S(1)} collective-permute-done((bf16[512,256]{1,0:T(8,128)(2,1)S(1)}, bf16[512,256]{1,0:T(8,128)(2,1)S(1)}, u32[]{:S(2)}, u32[]{:S(2)}) %collective-permute-start.47) | collective-permute-done | bytes 262176 | tf_op jit(solution)/shard_map/ppermute | solution.py:567
  237.0 2.4 collective-permute-start.49
  242.0 3.1 %collective-permute-done.50 = f32[3,2176]{1,0:T(4,128)S(1)} collective-permute-done((f32[3,2176]{1,0:T(4,128)S(1)}, f32[3,2176]{1,0:T(4,128)S(1)}, u32[]{:S(2)}, u32[]{:S(2)}) %collective-permute-start.50) | collective-permute-done | bytes 26144 | tf_op jit(solution)/shard_map/ppermute | solution.py:577
  247.2 2.2 share.2
  249.8 2.2 grad_pred.1
  253.7 25.6 %backward.1 = (f32[8192,512]{1,0:T(8,128)}, f32[64,128]{1,0:T(8,128)S(1)}) custom-call(s32[8]{0:T(128)S(1)} %pad_add_fusion.order_ref, f32[8192,512]{1,0:T(8,128)} %logits_ref.5, f32[64,128]{1,0:T(8,128)S(1)} %convert_bitcast_fusion.enable_ref, f32[64,128]{1,0:T(8,128)S(1)} %get-tuple-element.382.retain_ref, f32[3,512]{1,0:T(4,128)S(1)} %get-tuple-element.336.col_ref, ...), custom_call_target="tpu_custom_call" | custom-call | flops 1 | bytes 1 | tf_op jit(solution)/shard_map/backward/pallas_call | solution.py:402
  279.4 2.6 collective-permute-start.57
  283.8 2.7 share.3
  (263 shorter events, 93.9 us)
Async XLA Ops:
  2.0 26.4 %collective-permute-start.1 = (bf16[1024,512]{1,0:T(8,128)(2,1)S(1)}, bf16[1024,512]{1,0:T(8,128)(2,1)}, u32[]{:S(2)}, u32[]{:S(2)}) collective-permute-start(bf16[1024,512]{1,0:T(8,128)(2,1)S(1)} %slice.47), channel_id=1, source_target_pairs={{0,4},{2,6},{4,0},{6,2},{8,12},{10,14},{12,8},{14,10},{1,5},{3,7},... | collective-permute-start | bytes 3145736 | tf_op jit(solution)/shard_map/ppermute | solution.py:648
  5.0 23.3 %collective-permute-start.2 = (bf16[1024,512]{1,0:T(8,128)(2,1)S(1)}, bf16[1024,512]{1,0:T(8,128)(2,1)S(1)}, u32[]{:S(2)}, u32[]{:S(2)}) collective-permute-start(bf16[1024,512]{1,0:T(8,128)(2,1)S(1)} %slice.47), channel_id=1, source_target_pairs={{4,8},{6,10},{8,4},{10,6},{5,9},{7,11},{9,5},{11,7},{20,24},{22,26... | collective-permute-start | bytes 3145736 | tf_op jit(solution)/shard_map/ppermute | solution.py:651
  5.8 48.4 %collective-permute-start = (bf16[1024,1024]{1,0:T(8,128)(2,1)}, bf16[1024,1024]{1,0:T(8,128)(2,1)}, u32[]{:S(2)}, u32[]{:S(2)}) collective-permute-start(bf16[1024,1024]{1,0:T(8,128)(2,1)} %refs_0_.5), channel_id=1, source_target_pairs={{0,2},{2,0},{4,6},{6,4},{8,10},{10,8},{12,14},{14,12},{1,3},{3,1},... | collective-permute-start | bytes 6291464 | tf_op jit(solution)/shard_map/ppermute | solution.py:654
  7.4 48.0 %collective-permute-start.6 = (bf16[1024,1024]{1,0:T(8,128)(2,1)}, bf16[1024,1024]{1,0:T(8,128)(2,1)}, u32[]{:S(2)}, u32[]{:S(2)}) collective-permute-start(bf16[1024,1024]{1,0:T(8,128)(2,1)} %refs_0_.5), channel_id=1, source_target_pairs={{0,1},{1,0},{2,3},{3,2},{4,5},{5,4},{6,7},{7,6},{8,9},{9,8},{10,11... | collective-permute-start | bytes 6291464 | tf_op jit(solution)/shard_map/ppermute | solution.py:571
  9.4 14.8 %collective-permute-start.3 = (f32[512,256]{1,0:T(8,128)S(1)}, f32[512,256]{1,0:T(8,128)S(1)}, u32[]{:S(2)}, u32[]{:S(2)}) collective-permute-start(f32[512,256]{1,0:T(8,128)S(1)} %get-tuple-element.380), channel_id=1, source_target_pairs={{0,1},{1,0},{2,3},{3,2},{4,5},{5,4},{6,7},{7,6},{8,9},{9,8},{10,11... | collective-permute-start | bytes 1572872 | tf_op jit(solution)/shard_map/ppermute | solution.py:571
  28.3 27.0 %collective-permute-start.4 = (bf16[1024,512]{1,0:T(8,128)(2,1)S(1)}, bf16[1024,512]{1,0:T(8,128)(2,1)S(1)}, u32[]{:S(2)}, u32[]{:S(2)}) collective-permute-start(bf16[1024,512]{1,0:T(8,128)(2,1)S(1)} %collective-permute-done.2.b_ref), channel_id=1, source_target_pairs={{0,4},{2,6},{4,0},{6,2},{8,12},{10,14},{12,8},{14,10},{1,5},{3,7},... | collective-permute-start | bytes 3145736 | tf_op jit(solution)/shard_map/ppermute | solution.py:648
  33.0 22.4 %collective-permute-start.5 = (bf16[1024,512]{1,0:T(8,128)(2,1)}, bf16[1024,512]{1,0:T(8,128)(2,1)}, u32[]{:S(2)}, u32[]{:S(2)}) collective-permute-start(bf16[1024,512]{1,0:T(8,128)(2,1)} %collective-permute-done.1.refs_1_), channel_id=1, source_target_pairs={{4,8},{6,10},{8,4},{10,6},{5,9},{7,11},{9,5},{11,7},{20,24},{22,26... | collective-permute-start | bytes 3145736 | tf_op jit(solution)/shard_map/ppermute | solution.py:651
  38.3 15.8 %collective-permute-start.8 = (f32[512,256]{1,0:T(8,128)}, f32[512,256]{1,0:T(8,128)S(1)}, u32[]{:S(2)}, u32[]{:S(2)}) collective-permute-start(f32[512,256]{1,0:T(8,128)} %get-tuple-element.192), channel_id=1, source_target_pairs={{0,1},{1,0},{2,3},{3,2},{4,5},{5,4},{6,7},{7,6},{8,9},{9,8},{10,11... | collective-permute-start | bytes 1572872 | tf_op jit(solution)/shard_map/ppermute | solution.py:571
  55.4 25.7 %collective-permute-start.10 = (bf16[1024,512]{1,0:T(8,128)(2,1)}, bf16[1024,512]{1,0:T(8,128)(2,1)}, u32[]{:S(2)}, u32[]{:S(2)}) collective-permute-start(bf16[1024,512]{1,0:T(8,128)(2,1)} %collective-permute-done.5.c_ref), channel_id=1, source_target_pairs={{0,4},{2,6},{4,0},{6,2},{8,12},{10,14},{12,8},{14,10},{1,5},{3,7},... | collective-permute-start | bytes 3145736 | tf_op jit(solution)/shard_map/ppermute | solution.py:648
  59.3 23.5 %collective-permute-start.9 = (bf16[1024,512]{1,0:T(8,128)(2,1)}, bf16[1024,512]{1,0:T(8,128)(2,1)}, u32[]{:S(2)}, u32[]{:S(2)}) collective-permute-start(bf16[1024,512]{1,0:T(8,128)(2,1)} %collective-permute-done.1.refs_1_), channel_id=1, source_target_pairs={{0,2},{2,0},{4,6},{6,4},{8,10},{10,8},{12,14},{14,12},{1,3},{3,1},... | collective-permute-start | bytes 3145736 | tf_op jit(solution)/shard_map/ppermute | solution.py:654
  60.8 22.0 %collective-permute-start.11 = (bf16[1024,512]{1,0:T(8,128)(2,1)}, bf16[1024,512]{1,0:T(8,128)(2,1)}, u32[]{:S(2)}, u32[]{:S(2)}) collective-permute-start(bf16[1024,512]{1,0:T(8,128)(2,1)} %collective-permute-done.1.refs_1_), channel_id=1, source_target_pairs={{0,1},{1,0},{2,3},{3,2},{4,5},{5,4},{6,7},{7,6},{8,9},{9,8},{10,11... | collective-permute-start | bytes 3145736 | tf_op jit(solution)/shard_map/ppermute | solution.py:571
  60.8 25.9 %collective-permute-start.17 = (bf16[1024,1024]{1,0:T(8,128)(2,1)}, bf16[1024,1024]{1,0:T(8,128)(2,1)}, u32[]{:S(2)}, u32[]{:S(2)}) collective-permute-start(bf16[1024,1024]{1,0:T(8,128)(2,1)} %collective-permute-done.refs_1_.refs_3_), channel_id=1, source_target_pairs={{0,1},{1,0},{2,3},{3,2},{4,5},{5,4},{6,7},{7,6},{8,9},{9,8},{10,11... | collective-permute-start | bytes 6291464 | tf_op jit(solution)/shard_map/ppermute | solution.py:571
  61.3 21.5 %collective-permute-start.12 = (bf16[1024,384]{1,0:T(8,128)(2,1)}, bf16[1024,384]{1,0:T(8,128)(2,1)}, u32[]{:S(2)}, u32[]{:S(2)}) collective-permute-start(bf16[1024,384]{1,0:T(8,128)(2,1)} %slice.49), channel_id=1, source_target_pairs={{4,8},{6,10},{8,4},{10,6},{5,9},{7,11},{9,5},{11,7},{20,24},{22,26... | collective-permute-start | bytes 2359304 | tf_op jit(solution)/shard_map/ppermute | solution.py:651
  82.9 22.6 %collective-permute-start.13 = (bf16[2048,256]{1,0:T(8,128)(2,1)S(1)}, bf16[2048,256]{1,0:T(8,128)(2,1)S(1)}, u32[]{:S(2)}, u32[]{:S(2)}) collective-permute-start(bf16[2048,256]{1,0:T(8,128)(2,1)S(1)} %get-tuple-element.200.refs_2_), channel_id=1, source_target_pairs={{0,2},{2,0},{4,6},{6,4},{8,10},{10,8},{12,14},{14,12},{1,3},{3,1},... | collective-permute-start | bytes 3145736 | tf_op jit(solution)/shard_map/ppermute | solution.py:654
  84.4 21.1 %collective-permute-start.15 = (bf16[2048,256]{1,0:T(8,128)(2,1)S(1)}, bf16[2048,256]{1,0:T(8,128)(2,1)S(1)}, u32[]{:S(2)}, u32[]{:S(2)}) collective-permute-start(bf16[2048,256]{1,0:T(8,128)(2,1)S(1)} %get-tuple-element.200.refs_2_), channel_id=1, source_target_pairs={{0,1},{1,0},{2,3},{3,2},{4,5},{5,4},{6,7},{7,6},{8,9},{9,8},{10,11... | collective-permute-start | bytes 3145736 | tf_op jit(solution)/shard_map/ppermute | solution.py:571
  84.4 21.1 %collective-permute-start.16 = (bf16[1024,512]{1,0:T(8,128)(2,1)}, bf16[1024,512]{1,0:T(8,128)(2,1)S(1)}, u32[]{:S(2)}, u32[]{:S(2)}) collective-permute-start(bf16[1024,512]{1,0:T(8,128)(2,1)} %collective-permute-done.9.refs_4_), channel_id=1, source_target_pairs={{0,1},{1,0},{2,3},{3,2},{4,5},{5,4},{6,7},{7,6},{8,9},{9,8},{10,11... | collective-permute-start | bytes 3145736 | tf_op jit(solution)/shard_map/ppermute | solution.py:571
  84.9 19.7 %collective-permute-start.14 = (bf16[1024,384]{1,0:T(8,128)(2,1)}, bf16[1024,384]{1,0:T(8,128)(2,1)S(1)}, u32[]{:S(2)}, u32[]{:S(2)}) collective-permute-start(bf16[1024,384]{1,0:T(8,128)(2,1)} %slice.49), channel_id=1, source_target_pairs={{0,4},{2,6},{4,0},{6,2},{8,12},{10,14},{12,8},{14,10},{1,5},{3,7},... | collective-permute-start | bytes 2359304 | tf_op jit(solution)/shard_map/ppermute | solution.py:648
  105.6 25.6 %collective-permute-start.18 = (bf16[2048,256]{1,0:T(8,128)(2,1)S(1)}, bf16[2048,256]{1,0:T(8,128)(2,1)S(1)}, u32[]{:S(2)}, u32[]{:S(2)}) collective-permute-start(bf16[2048,256]{1,0:T(8,128)(2,1)S(1)} %get-tuple-element.216.refs_2_), channel_id=1, source_target_pairs={{0,2},{2,0},{4,6},{6,4},{8,10},{10,8},{12,14},{14,12},{1,3},{3,1},... | collective-permute-start | bytes 3145736 | tf_op jit(solution)/shard_map/ppermute | solution.py:654
  107.2 24.0 %collective-permute-start.22 = (bf16[2048,256]{1,0:T(8,128)(2,1)S(1)}, bf16[2048,256]{1,0:T(8,128)(2,1)S(1)}, u32[]{:S(2)}, u32[]{:S(2)}) collective-permute-start(bf16[2048,256]{1,0:T(8,128)(2,1)S(1)} %get-tuple-element.216.refs_2_), channel_id=1, source_target_pairs={{0,1},{1,0},{2,3},{3,2},{4,5},{5,4},{6,7},{7,6},{8,9},{9,8},{10,11... | collective-permute-start | bytes 3145736 | tf_op jit(solution)/shard_map/ppermute | solution.py:571
  107.3 20.0 %collective-permute-start.19 = (bf16[1024,384]{1,0:T(8,128)(2,1)}, bf16[1024,384]{1,0:T(8,128)(2,1)S(1)}, u32[]{:S(2)}, u32[]{:S(2)}) collective-permute-start(bf16[1024,384]{1,0:T(8,128)(2,1)} %collective-permute-done.12.b_ref), channel_id=1, source_target_pairs={{0,4},{2,6},{4,0},{6,2},{8,12},{10,14},{12,8},{14,10},{1,5},{3,7},... | collective-permute-start | bytes 2359304 | tf_op jit(solution)/shard_map/ppermute | solution.py:648
  108.8 18.5 %collective-permute-start.20 = (bf16[1024,384]{1,0:T(8,128)(2,1)S(1)}, bf16[1024,384]{1,0:T(8,128)(2,1)S(1)}, u32[]{:S(2)}, u32[]{:S(2)}) collective-permute-start(bf16[1024,384]{1,0:T(8,128)(2,1)S(1)} %collective-permute-done.14.refs_0_), channel_id=1, source_target_pairs={{4,8},{6,10},{8,4},{10,6},{5,9},{7,11},{9,5},{11,7},{20,24},{22,26... | collective-permute-start | bytes 2359304 | tf_op jit(solution)/shard_map/ppermute | solution.py:651
  131.2 20.0 %collective-permute-start.23 = (bf16[1024,384]{1,0:T(8,128)(2,1)S(1)}, bf16[1024,384]{1,0:T(8,128)(2,1)S(1)}, u32[]{:S(2)}, u32[]{:S(2)}) collective-permute-start(bf16[1024,384]{1,0:T(8,128)(2,1)S(1)} %collective-permute-done.14.refs_0_), channel_id=1, source_target_pairs={{0,2},{2,0},{4,6},{6,4},{8,10},{10,8},{12,14},{14,12},{1,3},{3,1},... | collective-permute-start | bytes 2359304 | tf_op jit(solution)/shard_map/ppermute | solution.py:654
  132.8 19.6 %collective-permute-start.24 = (bf16[1024,384]{1,0:T(8,128)(2,1)S(1)}, bf16[1024,384]{1,0:T(8,128)(2,1)S(1)}, u32[]{:S(2)}, u32[]{:S(2)}) collective-permute-start(bf16[1024,384]{1,0:T(8,128)(2,1)S(1)} %collective-permute-done.20.c_ref), channel_id=1, source_target_pairs={{0,4},{2,6},{4,0},{6,2},{8,12},{10,14},{12,8},{14,10},{1,5},{3,7},... | collective-permute-start | bytes 2359304 | tf_op jit(solution)/shard_map/ppermute | solution.py:648
  134.3 18.1 %collective-permute-start.27 = (bf16[1024,384]{1,0:T(8,128)(2,1)S(1)}, bf16[1024,384]{1,0:T(8,128)(2,1)S(1)}, u32[]{:S(2)}, u32[]{:S(2)}) collective-permute-start(bf16[1024,384]{1,0:T(8,128)(2,1)S(1)} %collective-permute-done.14.refs_0_), channel_id=1, source_target_pairs={{0,1},{1,0},{2,3},{3,2},{4,5},{5,4},{6,7},{7,6},{8,9},{9,8},{10,11... | collective-permute-start | bytes 2359304 | tf_op jit(solution)/shard_map/ppermute | solution.py:571
  134.3 14.3 %collective-permute-start.26 = (bf16[512,512]{1,0:T(8,128)(2,1)S(1)}, bf16[512,512]{1,0:T(8,128)(2,1)S(1)}, u32[]{:S(2)}, u32[]{:S(2)}) collective-permute-start(bf16[512,512]{1,0:T(8,128)(2,1)S(1)} %get-tuple-element.230.refs_0_), channel_id=1, source_target_pairs={{0,16},{16,0},{1,17},{17,1},{2,18},{18,2},{3,19},{19,3},{4,20},{20... | collective-permute-start | bytes 1572872 | tf_op jit(solution)/shard_map/ppermute | solution.py:567
  157.9 24.7 %collective-permute-start.35 = (f32[512,512]{1,0:T(8,128)S(1)}, f32[512,512]{1,0:T(8,128)S(1)}, u32[]{:S(2)}, u32[]{:S(2)}) collective-permute-start(f32[512,512]{1,0:T(8,128)S(1)} %get-tuple-element.258.refs_0_), channel_id=1, source_target_pairs={{0,16},{16,0},{1,17},{17,1},{2,18},{18,2},{3,19},{19,3},{4,20},{20... | collective-permute-start | bytes 3145736 | tf_op jit(solution)/shard_map/ppermute | solution.py:567
  168.2 30.5 %collective-permute-start.36 = (bf16[2064,256]{1,0:T(8,128)(2,1)S(1)}, bf16[2064,256]{1,0:T(8,128)(2,1)}, u32[]{:S(2)}, u32[]{:S(2)}) collective-permute-start(bf16[2064,256]{1,0:T(8,128)(2,1)S(1)} %get-tuple-element.280.refs_0_), channel_id=1, source_target_pairs={{0,2},{2,0},{4,6},{6,4},{8,10},{10,8},{12,14},{14,12},{1,3},{3,1},... | collective-permute-start | bytes 3170312 | tf_op jit(solution)/shard_map/ppermute | solution.py:654
  183.7 15.0 %collective-permute-start.37 = (bf16[2048,128]{1,0:T(8,128)(2,1)}, bf16[2048,128]{1,0:T(8,128)(2,1)}, u32[]{:S(2)}, u32[]{:S(2)}) collective-permute-start(bf16[2048,128]{1,0:T(8,128)(2,1)} %collective-permute-done.29.b_ref), channel_id=1, source_target_pairs={{0,4},{2,6},{4,0},{6,2},{8,12},{10,14},{12,8},{14,10},{1,5},{3,7},... | collective-permute-start | bytes 1572872 | tf_op jit(solution)/shard_map/ppermute | solution.py:648
  198.7 15.8 %collective-permute-start.43 = (f32[512,512]{1,0:T(8,128)S(1)}, f32[512,512]{1,0:T(8,128)S(1)}, u32[]{:S(2)}, u32[]{:S(2)}) collective-permute-start(f32[512,512]{1,0:T(8,128)S(1)} %dynamic-slice.2), channel_id=1, source_target_pairs={{0,1},{1,0},{2,3},{3,2},{4,5},{5,4},{6,7},{7,6},{8,9},{9,8},{10,11... | collective-permute-start | bytes 3145736 | tf_op jit(solution)/shard_map/ppermute | solution.py:571
  216.2 14.8 %collective-permute-start.46 = (bf16[512,512]{1,0:T(8,128)(2,1)S(1)}, bf16[512,512]{1,0:T(8,128)(2,1)S(1)}, u32[]{:S(2)}, u32[]{:S(2)}) collective-permute-start(bf16[512,512]{1,0:T(8,128)(2,1)S(1)} %get-tuple-element.306.refs_0_), channel_id=1, source_target_pairs={{0,16},{16,0},{1,17},{17,1},{2,18},{18,2},{3,19},{19,3},{4,20},{20... | collective-permute-start | bytes 1572872 | tf_op jit(solution)/shard_map/ppermute | solution.py:567
  251.9 27.3 %collective-permute-start.54 = (f32[512,512]{1,0:T(8,128)S(1)}, f32[512,512]{1,0:T(8,128)S(1)}, u32[]{:S(2)}, u32[]{:S(2)}) collective-permute-start(f32[512,512]{1,0:T(8,128)S(1)} %get-tuple-element.349), channel_id=1, source_target_pairs={{0,1},{1,0},{2,3},{3,2},{4,5},{5,4},{6,7},{7,6},{8,9},{9,8},{10,11... | collective-permute-start | bytes 3145736 | tf_op jit(solution)/shard_map/ppermute | solution.py:571
  252.2 27.1 %collective-permute-start.55 = (bf16[512,1024]{1,0:T(8,128)(2,1)S(1)}, bf16[512,1024]{1,0:T(8,128)(2,1)S(1)}, u32[]{:S(2)}, u32[]{:S(2)}) collective-permute-start(bf16[512,1024]{1,0:T(8,128)(2,1)S(1)} %copy-done.29), channel_id=1, source_target_pairs={{0,16},{16,0},{1,17},{17,1},{2,18},{18,2},{3,19},{19,3},{4,20},{20... | collective-permute-start | bytes 3145736 | tf_op jit(solution)/shard_map/ppermute | solution.py:567
  (85 other events, 744.2 us)

commit v2 on v1

--- a/solution.py
+++ b/solution.py
@@ -292,8 +292,8 @@
 
 def grad_pred_kernel(widths, genes_total, spots_total, core_ref, spot_ref, gene_ref, cols_ref, own_ref, *refs):
     n = len(widths)
-    other_refs, pred_refs = refs[:3], refs[3 : 3 + n]
-    refs = refs[3:]
+    other_refs, pred_refs = refs[:4], refs[4 : 4 + n]
+    refs = refs[4:]
     quarter = other_refs[0].shape[1]
     turned_ref, col_ref, sums_ref = refs[n:]
     spot = spot_ref[...]
@@ -313,8 +313,8 @@
     for q in range(n):
         wide = widths[q]
         pred = pred_refs[q][...]
-        other = other_refs[min(low // quarter, 2)]
-        other_low = low - min(low // quarter, 2) * quarter
+        other = other_refs[low // quarter]
+        other_low = low % quarter
         target = in_order(core_ref[0], own_ref[:, low : low + wide], other[:, other_low : other_low + wide])
         cols = slice(at, at + 2 * wide)
         grad = pred * (gene_pred[:, cols] + spot_pred) - target * (gene_target[:, cols] + spot_target)
@@ -349,7 +349,7 @@
             grid=(1,),
             in_specs=[VMEM] * 3
             + [pl.BlockSpec((spots, half), lambda i, core: (core[0], 0))]
-            + [VMEM] * (3 + len(preds)),
+            + [VMEM] * (4 + len(preds)),
             out_specs=[VMEM] * 3,
         ),
         out_shape=[
@@ -596,7 +596,7 @@
         self.target = spot_expression
         sent = lax.dynamic_slice_in_dim(spot_expression, (1 - self.core) * self.spots, self.spots, 0)
         quarter = self.half // 4
-        self.target_sent = [sent[:, :quarter], sent[:, quarter : 2 * quarter], sent[:, 2 * quarter :]]
+        self.target_sent = [sent[:, k * quarter : (k + 1) * quarter] for k in range(4)]
 
     def local_stats(self):
         part = col_stats(self.logits, self.enable, self.retain)
@@ -619,8 +619,8 @@
         return mapped_turned(order, logits, self.enable, self.retain, shift)
 
     def stats(self, parts, other, at, wide, part=0):
-        begin = self.half - other.shape[1] if other.shape[1] > self.half // 4 else at // (self.half // 4) * (self.half // 4)
-        return pred_stats(self.core_flag, parts, self.target, other, at // wide, (at - begin) // wide, wide, part)
+        column = at % (self.half // 4) // wide
+        return pred_stats(self.core_flag, parts, self.target, other, at // wide, column, wide, part)
 
     def gathered_whole(self):
         own = lax.all_gather(self.expression, "spots", axis=0, tiled=True)
@@ -636,7 +636,7 @@
             pieces = tuple((r, 0, r, q) for r in range(PIECES))
             (partial,), (panel,) = forward(self.core_flag, mapped, [(own, other)], [pieces], wide)
             panels.append(panel)
-            stats.append(self.stats([lax.psum(partial, "cells")], self.target_other[min(q, 2)], q * wide, wide))
+            stats.append(self.stats([lax.psum(partial, "cells")], self.target_other[q], q * wide, wide))
         return order, widths, panels, stats, (), None
 
     def gathered_line(self):
@@ -750,18 +750,21 @@
             [(m2, m2_o), (ym2, ym2_o)], [rest(0)], 1, (more[0:1], more[3:4]), near=True, column=0, columns=4
         )
         stats0 = self.stats([high0, high0_away], target_0, 0, 2 * unit)
-        cf, high2, away1, m34, bf, af, *stats0 = hold(cf, high2, away1, m34, bf, af, *stats0)
+        cf, high2, away1, m34, bf, af, target_2, *stats0 = hold(
+            cf, high2, away1, m34, bf, af, self.target_sent[2], *stats0
+        )
+        target_2 = swap_genes(target_2)
         ef, ff = near(bf), near(cf)
         m34_o = swap_genes(m34)
         high2_away = swap_cells(high2)
         stats1 = self.stats([partial1, away1], target_1, 2 * unit, 2 * unit)
-        ym34, ef, m34, mapped, high2_away, af, low0, target_2, *stats1 = hold(
-            ym34, ef, m34, mapped, high2_away, af, low0, self.target_sent[2], *stats1
+        ym34, ef, m34, mapped, high2_away, af, low0, target_2, target_3, *stats1 = hold(
+            ym34, ef, m34, mapped, high2_away, af, low0, target_2, self.target_sent[3], *stats1
         )
         ym34_o, af_o = swap_genes(ym34), swap_genes(af)
         low0_away = swap_cells(low0)
-        target_2 = swap_genes(target_2)
-        self.target_other = (target_0, target_1, target_2)
+        target_3 = swap_genes(target_3)
+        self.target_other = (target_0, target_1, target_2, target_3)
         (high34, low), (panel3, panel4) = run(
             [(m34, m34_o), (ym34, ym34_o)],
             [rest(0), rest(1)],
@@ -771,13 +774,13 @@
             columns=4,
             left=low,
         )
-        ff, high34, low0_away, target_2, af_o, mapped = hold(ff, high34, low0_away, target_2, af_o, mapped)
+        ff, high34, low0_away, target_3, af_o, mapped = hold(ff, high34, low0_away, target_3, af_o, mapped)
         high34_away = swap_cells(high34)
         (mff,) = pick(bf, ef, cf, ff, 1)
         mff_o = swap_genes(mff)
         late = ((1, 0, 0, 0), (2, 1, 0, 0), (3, 1, 2, 0), (5, 0, 1, 0), (6, 1, 1, 0), (7, 1, 3, 0))
         (highf, low), (panelf,) = run(
-            [(af, af_o), (mff, mff_o)], [late], 1, (begun[3:4], begun[7:8]), column=3, columns=4, left=low
+            [(af, af_o), (mff, mff_o)], [late], 1, (begun[3:4], begun[7:8]), column=3, columns=4, left=low, near=True
         )
         highf, high2, high2_away = hold(highf, high2, high2_away)
         highf_away = swap_cells(highf)
@@ -785,8 +788,8 @@
         late = [
             self.stats([high2, high2_away], target_2, 4 * unit, unit),
             self.stats([high34, high34_away], target_2, 5 * unit, unit),
-            self.stats([high34, high34_away], target_2, 6 * unit, unit, 1),
-            self.stats([highf, highf_away], target_2, 7 * unit, unit),
+            self.stats([high34, high34_away], target_3, 6 * unit, unit, 1),
+            self.stats([highf, highf_away], target_3, 7 * unit, unit),
         ]
         widths = (2 * unit,) * 2 + (unit,) * 4
         panels = (panel0, panel1, panel2, panel3, panel4, panelf)

time: 295 us -> 292 us (0.990)
  local copies, waits for them, and re-layouts: 23.1 us -> 14.9 us
  waiting for transfers between devices: 71.8 us -> 79.7 us
  Pallas kernels: 125 us -> 122 us
    unnamed x115 -> x89, local copies, waits for them, and re-layouts: 13.5 us -> 6.02 us
    ppermute x8, waiting for transfers between devices: 16 us -> 23.3 us  [swap_cells(): return lax.ppermute(x, 'cells', [(0, 1), (1, 0)])]
  transfers between devices with their start and end apart: 63 -> 64, of which waited for: 25 -> 25; matrix products, arithmetic and copies ran while one was open for 4% -> 4% of each run, Pallas kernels for 41% -> 41%
where the time goes in v2:
time: 292 us; the launch traced here: 291 us
  Pallas kernels  122 us (42%)
  waiting for transfers between devices  79.7 us (27%)
  starting transfers between devices  68.8 us (24%)
  local copies, waits for them, and re-layouts  14.9 us (5%)
  other arithmetic  3.71 us (1%)
    pallas_call x7, Pallas kernels, forward(): pl.pallas_call(functools.partial(forward_kernel, chunks, len(own), rows,...  53.6 us
    ppermute x9, waiting for transfers between devices, near(): return lax.ppermute(x, 'spots', near_pairs)  39.9 us
    pallas_call x1, Pallas kernels, backward(): pl.pallas_call(functools.partial(backward_kernel, widths), grid_spec=pltp...  25.6 us
    ppermute x9, starting transfers between devices, near(): return lax.ppermute(x, 'spots', near_pairs)  25 us
    ppermute x8, waiting for transfers between devices, swap_cells(): return lax.ppermute(x, 'cells', [(0, 1), (1, 0)])  23.3 us
    pallas_call x1, Pallas kernels, mapped_turned(): pl.pallas_call(mapped_kernel, grid_spec=pltpu.PrefetchScalarGridSpec(num_...  15.6 us
    ppermute x8, starting transfers between devices, swap_cells(): return lax.ppermute(x, 'cells', [(0, 1), (1, 0)])  12.1 us
    pallas_call x1, Pallas kernels, col_stats(): pl.pallas_call(col_stats_kernel, grid=(cells // block,), in_specs=[pl.Blo...  10.9 us
  transfers between devices with their start and end apart: 64, of which 25 were waited for; matrix products, arithmetic and copies ran while one was open for 4% of the time, Pallas kernels for 41%

profile of v2, /device:TPU:0, one launch (start us, length us, event | category | flops | bytes accessed | tf_op | source)
XLA Modules:
  0.0 290.7 jit_solution(855802228889884310)
XLA Ops:
  2.0 3.1 %collective-permute-start.1 = (bf16[1024,512]{1,0:T(8,128)(2,1)S(1)}, bf16[1024,512]{1,0:T(8,128)(2,1)}, u32[]{:S(2)}, u32[]{:S(2)}) collective-permute-start(bf16[1024,512]{1,0:T(8,128)(2,1)S(1)} %slice.50), channel_id=1, source_target_pairs={{0,4},{2,6},{4,0},{6,2},{8,12},{10,14},{12,8},{14,10},{1,5},{3,7},... | collective-permute-start | bytes 3145736 | tf_op jit(solution)/shard_map/ppermute | solution.py:648
  7.4 2.7 fusion.4
  11.2 10.9 %col_stats.1 = f32[3,512]{1,0:T(4,128)S(1)} custom-call(f32[8192,512]{1,0:T(8,128)} %logits_ref.5, f32[64,128]{1,0:T(8,128)S(1)} %convert_bitcast_fusion.enable_ref, f32[64,128]{1,0:T(8,128)S(1)} %get-tuple-element.388.retain_ref), custom_call_target="tpu_custom_call" | custom-call | flops 1 | bytes 1 | tf_op jit(solution)/shard_map/col_stats/pallas_call | solution.py:76
  24.9 3.4 %collective-permute-done.1.refs_1_ = bf16[1024,512]{1,0:T(8,128)(2,1)} collective-permute-done((bf16[1024,512]{1,0:T(8,128)(2,1)S(1)}, bf16[1024,512]{1,0:T(8,128)(2,1)}, u32[]{:S(2)}, u32[]{:S(2)}) %collective-permute-start.1) | collective-permute-done | bytes 1048608 | tf_op jit(solution)/shard_map/ppermute | solution.py:648
  28.3 4.7 %collective-permute-start.4 = (bf16[1024,512]{1,0:T(8,128)(2,1)S(1)}, bf16[1024,512]{1,0:T(8,128)(2,1)S(1)}, u32[]{:S(2)}, u32[]{:S(2)}) collective-permute-start(bf16[1024,512]{1,0:T(8,128)(2,1)S(1)} %collective-permute-done.2.b_ref), channel_id=1, source_target_pairs={{0,4},{2,6},{4,0},{6,2},{8,12},{10,14},{12,8},{14,10},{1,5},{3,7},... | collective-permute-start | bytes 3145736 | tf_op jit(solution)/shard_map/ppermute | solution.py:648
  36.2 2.2 collective-permute-done.7
  38.5 15.6 %mapped_turned.1.mapped_ref = bf16[512,8192]{1,0:T(8,128)(2,1)} custom-call(s32[8]{0:T(128)S(1)} %pad_add_fusion.order_ref, f32[8192,512]{1,0:T(8,128)} %logits_ref.5, f32[64,128]{1,0:T(8,128)S(1)} %convert_bitcast_fusion.enable_ref, f32[64,128]{1,0:T(8,128)S(1)} %get-tuple-element.388.retain_ref, f32[1,512]{1,0:T(1,128)S(1)} %get-tuple-element.390.shift_ref), custom_call_target="tpu_custom_call" | custom-call | flops 1 | bytes 1 | tf_op jit(solution)/shard_map/mapped_turned/pallas_call | solution.py:104
  55.4 3.9 %collective-permute-start.10 = (bf16[1024,512]{1,0:T(8,128)(2,1)}, bf16[1024,512]{1,0:T(8,128)(2,1)}, u32[]{:S(2)}, u32[]{:S(2)}) collective-permute-start(bf16[1024,512]{1,0:T(8,128)(2,1)} %collective-permute-done.5.c_ref), channel_id=1, source_target_pairs={{0,4},{2,6},{4,0},{6,2},{8,12},{10,14},{12,8},{14,10},{1,5},{3,7},... | collective-permute-start | bytes 3145736 | tf_op jit(solution)/shard_map/ppermute | solution.py:648
  65.6 15.5 %collective-permute-done.10.f_ref = bf16[1024,512]{1,0:T(8,128)(2,1)} collective-permute-done((bf16[1024,512]{1,0:T(8,128)(2,1)}, bf16[1024,512]{1,0:T(8,128)(2,1)}, u32[]{:S(2)}, u32[]{:S(2)}) %collective-permute-start.10) | collective-permute-done | bytes 1048608 | tf_op jit(solution)/shard_map/ppermute | solution.py:648
  86.7 8.4 %forward.7 = (f32[512,256]{1,0:T(8,128)S(1)}, f32[512,256]{1,0:T(8,128)S(1)}, f32[512,256]{1,0:T(8,128)S(1)}, f32[512,256]{1,0:T(8,128)S(1)}, bf16[8192,256]{1,0...) custom-call(s32[1]{0:T(128)} %bitcast.6.core_ref, ...), custom_call_target="tpu_custom_call" | custom-call | flops 1 | bytes 1 | tf_op jit(solution)/shard_map/forward/pallas_call | solution.py:218
  95.1 9.5 %collective-permute-done.14.refs_0_ = bf16[1024,384]{1,0:T(8,128)(2,1)S(1)} collective-permute-done((bf16[1024,384]{1,0:T(8,128)(2,1)}, bf16[1024,384]{1,0:T(8,128)(2,1)S(1)}, u32[]{:S(2)}, u32[]{:S(2)}) %collective-permute-start.14) | collective-permute-done | bytes 786464 | tf_op jit(solution)/shard_map/ppermute | solution.py:648
  110.7 9.9 %forward.8 = (bf16[512,512]{1,0:T(8,128)(2,1)S(1)}, bf16[512,512]{1,0:T(8,128)(2,1)}, bf16[8192,512]{1,0:T(8,128)(2,1)}) custom-call(s32[1]{0:T(128)} %bitcast.6.core_ref, bf16[512,8192]{1,0:T(8,128)(2,1)} %mapped_turned.1.mapped_ref, bf16[1024,1024]{1,0:T(8,128)(2,1)} %refs_0_.5, bf16[1024,512]{1,0:T(8,128)(2,1)} %collective-permute-done.1.refs_1_, ...), custom_call_target="tpu_custom_call" | custom-call | flops 1 | bytes 1 | tf_op jit(solution)/shard_map/forward/pallas_call | solution.py:218
  120.7 6.7 %collective-permute-done.19.e_ref = bf16[1024,384]{1,0:T(8,128)(2,1)S(1)} collective-permute-done((bf16[1024,384]{1,0:T(8,128)(2,1)}, bf16[1024,384]{1,0:T(8,128)(2,1)S(1)}, u32[]{:S(2)}, u32[]{:S(2)}) %collective-permute-start.19) | collective-permute-done | bytes 786464 | tf_op jit(solution)/shard_map/ppermute | solution.py:648
  127.3 3.8 %collective-permute-done.18.refs_5_ = bf16[2048,256]{1,0:T(8,128)(2,1)S(1)} collective-permute-done((bf16[2048,256]{1,0:T(8,128)(2,1)S(1)}, bf16[2048,256]{1,0:T(8,128)(2,1)S(1)}, u32[]{:S(2)}, u32[]{:S(2)}) %collective-permute-start.18) | collective-permute-done | bytes 1048608 | tf_op jit(solution)/shard_map/ppermute | solution.py:654
  138.8 9.4 %forward.9 = (f32[512,512]{1,0:T(8,128)S(1)}, bf16[8192,512]{1,0:T(8,128)(2,1)}) custom-call(s32[1]{0:T(128)} %bitcast.6.core_ref, bf16[512,8192]{1,0:T(8,128)(2,1)} %mapped_turned.1.mapped_ref, bf16[1024,1024]{1,0:T(8,128)(2,1)} %refs_0_.5, bf16[1024,512]{1,0:T(8,128)(2,1)} %collective-permute-done.1.refs_1_, bf16[2048,256]{1,0:T(8,128)(2,1)} %copy-done.12, ...), custom_call_target="tpu_custom_call" | custom-call | flops 1 | bytes 1 | tf_op jit(solution)/shard_map/forward/pallas_call | solution.py:218
  148.6 2.6 collective-permute-done.23.refs_1_
  159.6 6.6 %forward.10 = (f32[512,256]{1,0:T(8,128)S(1)}, f32[512,256]{1,0:T(8,128)S(1)}, f32[512,256]{1,0:T(8,128)S(1)}, bf16[8192,256]{1,0:T(8,128)(2,1)}, bf16[8192,256]{1,0:T(8,128)(2,1)}, /*index=5*/bf16[8192,256]{1,0:T(8,128)(2,1)}) custom-call(s32[1]{0:T(128)} %bitcast.6.core_ref, ...), custom_call_target="tpu_custom_call", output_to_operand_aliasing={{3}: (9, {}), {4}: (10, {}), {5}: (11, {})} | custom-call | flops 1 | bytes 1 | tf_op jit(solution)/shard_map/forward/pallas_call | solution.py:218
  171.5 4.9 %forward.11 = (bf16[512,256]{1,0:T(8,128)(2,1)S(1)}, bf16[512,1024]{1,0:T(8,128)(2,1)}, bf16[8192,256]{1,0:T(8,128)(2,1)}) custom-call(s32[1]{0:T(128)} %bitcast.6.core_ref, bf16[512,8192]{1,0:T(8,128)(2,1)} %mapped_turned.1.mapped_ref, bf16[2048,128]{1,0:T(8,128)(2,1)S(1)} %get-tuple-element.255.refs_0_, ...), custom_call_target="tpu_custom_call", output_to_operand_aliasing={{2}: (7, {})} | custom-call | flops 1 | bytes 1 | tf_op jit(solution)/shard_map/forward/pallas_call | solution.py:218
  176.4 5.5 %collective-permute-done.35.refs_1_ = f32[512,512]{1,0:T(8,128)S(1)} collective-permute-done((f32[512,512]{1,0:T(8,128)S(1)}, f32[512,512]{1,0:T(8,128)S(1)}, u32[]{:S(2)}, u32[]{:S(2)}) %collective-permute-start.35) | collective-permute-done | bytes 1048608 | tf_op jit(solution)/shard_map/ppermute | solution.py:567
  181.9 5.1 %collective-permute-start.37 = (bf16[2048,128]{1,0:T(8,128)(2,1)S(1)}, bf16[2048,128]{1,0:T(8,128)(2,1)S(1)}, u32[]{:S(2)}, u32[]{:S(2)}) collective-permute-start(bf16[2048,128]{1,0:T(8,128)(2,1)S(1)} %collective-permute-done.29.b_ref), channel_id=1, source_target_pairs={{0,4},{2,6},{4,0},{6,2},{8,12},{10,14},{12,8},{14,10},{1,5},{3,7},... | collective-permute-start | bytes 1572872 | tf_op jit(solution)/shard_map/ppermute | solution.py:648
  190.6 5.2 %collective-permute-done.38.refs_1_ = bf16[512,256]{1,0:T(8,128)(2,1)S(1)} collective-permute-done((bf16[512,256]{1,0:T(8,128)(2,1)S(1)}, bf16[512,256]{1,0:T(8,128)(2,1)S(1)}, u32[]{:S(2)}, u32[]{:S(2)}) %collective-permute-start.38) | collective-permute-done | bytes 262176 | tf_op jit(solution)/shard_map/ppermute | solution.py:567
  202.0 8.4 %forward.12 = (bf16[512,512]{1,0:T(8,128)(2,1)S(1)}, bf16[512,1024]{1,0:T(8,128)(2,1)}, bf16[8192,256]{1,0:T(8,128)(2,1)}, bf16[8192,256]{1,0:T(8,128)(2,1)}) custom-call(s32[1]{0:T(128)} %bitcast.6.core_ref, bf16[512,8192]{1,0:T(8,128)(2,1)} %mapped_turned.1.mapped_ref, ...), custom_call_target="tpu_custom_call", output_to_operand_aliasing={{2}: (8, {}), {3}: (9, {}), {1}: (10, {})} | custom-call | flops 1 | bytes 1 | tf_op jit(solution)/shard_map/forward/pallas_call | solution.py:218
  215.8 6.0 %forward.13 = (bf16[512,256]{1,0:T(8,128)(2,1)S(1)}, bf16[512,1024]{1,0:T(8,128)(2,1)}, bf16[8192,256]{1,0:T(8,128)(2,1)}) custom-call(s32[1]{0:T(128)} %bitcast.6.core_ref, bf16[512,8192]{1,0:T(8,128)(2,1)} %mapped_turned.1.mapped_ref, bf16[2048,128]{1,0:T(8,128)(2,1)S(1)} %collective-permute-done.28.refs_0_, ...), custom_call_target="tpu_custom_call", output_to_operand_aliasing={{2}: (7, {}), {1}: (8, {})} | custom-call | flops 1 | bytes 1 | tf_op jit(solution)/shard_map/forward/pallas_call | solution.py:218
  223.8 4.1 %collective-permute-done.47.refs_1_ = bf16[512,512]{1,0:T(8,128)(2,1)S(1)} collective-permute-done((bf16[512,512]{1,0:T(8,128)(2,1)S(1)}, bf16[512,512]{1,0:T(8,128)(2,1)S(1)}, u32[]{:S(2)}, u32[]{:S(2)}) %collective-permute-start.47) | collective-permute-done | bytes 524320 | tf_op jit(solution)/shard_map/ppermute | solution.py:567
  228.7 4.4 %collective-permute-done.48.refs_1_ = bf16[512,256]{1,0:T(8,128)(2,1)S(1)} collective-permute-done((bf16[512,256]{1,0:T(8,128)(2,1)S(1)}, bf16[512,256]{1,0:T(8,128)(2,1)S(1)}, u32[]{:S(2)}, u32[]{:S(2)}) %collective-permute-start.48) | collective-permute-done | bytes 262176 | tf_op jit(solution)/shard_map/ppermute | solution.py:567
  233.9 2.5 collective-permute-start.50
  238.9 3.1 %collective-permute-done.51 = f32[3,2176]{1,0:T(4,128)S(1)} collective-permute-done((f32[3,2176]{1,0:T(4,128)S(1)}, f32[3,2176]{1,0:T(4,128)S(1)}, u32[]{:S(2)}, u32[]{:S(2)}) %collective-permute-start.51) | collective-permute-done | bytes 26144 | tf_op jit(solution)/shard_map/ppermute | solution.py:577
  244.1 2.2 share.2
  246.7 2.2 grad_pred.1
  250.6 25.6 %backward.1 = (f32[8192,512]{1,0:T(8,128)}, f32[64,128]{1,0:T(8,128)S(1)}) custom-call(s32[8]{0:T(128)S(1)} %pad_add_fusion.order_ref, f32[8192,512]{1,0:T(8,128)} %logits_ref.5, f32[64,128]{1,0:T(8,128)S(1)} %convert_bitcast_fusion.enable_ref, f32[64,128]{1,0:T(8,128)S(1)} %get-tuple-element.388.retain_ref, f32[3,512]{1,0:T(4,128)S(1)} %get-tuple-element.340.col_ref, ...), custom_call_target="tpu_custom_call" | custom-call | flops 1 | bytes 1 | tf_op jit(solution)/shard_map/backward/pallas_call | solution.py:402
  276.4 2.6 collective-permute-start.58
  280.7 2.7 share.3
  (238 shorter events, 86.0 us)
Async XLA Ops:
  2.0 26.4 %collective-permute-start.1 = (bf16[1024,512]{1,0:T(8,128)(2,1)S(1)}, bf16[1024,512]{1,0:T(8,128)(2,1)}, u32[]{:S(2)}, u32[]{:S(2)}) collective-permute-start(bf16[1024,512]{1,0:T(8,128)(2,1)S(1)} %slice.50), channel_id=1, source_target_pairs={{0,4},{2,6},{4,0},{6,2},{8,12},{10,14},{12,8},{14,10},{1,5},{3,7},... | collective-permute-start | bytes 3145736 | tf_op jit(solution)/shard_map/ppermute | solution.py:648
  5.0 23.3 %collective-permute-start.2 = (bf16[1024,512]{1,0:T(8,128)(2,1)S(1)}, bf16[1024,512]{1,0:T(8,128)(2,1)S(1)}, u32[]{:S(2)}, u32[]{:S(2)}) collective-permute-start(bf16[1024,512]{1,0:T(8,128)(2,1)S(1)} %slice.50), channel_id=1, source_target_pairs={{4,8},{6,10},{8,4},{10,6},{5,9},{7,11},{9,5},{11,7},{20,24},{22,26... | collective-permute-start | bytes 3145736 | tf_op jit(solution)/shard_map/ppermute | solution.py:651
  5.8 48.4 %collective-permute-start = (bf16[1024,1024]{1,0:T(8,128)(2,1)}, bf16[1024,1024]{1,0:T(8,128)(2,1)}, u32[]{:S(2)}, u32[]{:S(2)}) collective-permute-start(bf16[1024,1024]{1,0:T(8,128)(2,1)} %refs_0_.5), channel_id=1, source_target_pairs={{0,2},{2,0},{4,6},{6,4},{8,10},{10,8},{12,14},{14,12},{1,3},{3,1},... | collective-permute-start | bytes 6291464 | tf_op jit(solution)/shard_map/ppermute | solution.py:654
  7.4 48.0 %collective-permute-start.6 = (bf16[1024,1024]{1,0:T(8,128)(2,1)}, bf16[1024,1024]{1,0:T(8,128)(2,1)}, u32[]{:S(2)}, u32[]{:S(2)}) collective-permute-start(bf16[1024,1024]{1,0:T(8,128)(2,1)} %refs_0_.5), channel_id=1, source_target_pairs={{0,1},{1,0},{2,3},{3,2},{4,5},{5,4},{6,7},{7,6},{8,9},{9,8},{10,11... | collective-permute-start | bytes 6291464 | tf_op jit(solution)/shard_map/ppermute | solution.py:571
  10.1 14.8 %collective-permute-start.3 = (f32[512,256]{1,0:T(8,128)S(1)}, f32[512,256]{1,0:T(8,128)S(1)}, u32[]{:S(2)}, u32[]{:S(2)}) collective-permute-start(f32[512,256]{1,0:T(8,128)S(1)} %get-tuple-element.386), channel_id=1, source_target_pairs={{0,1},{1,0},{2,3},{3,2},{4,5},{5,4},{6,7},{7,6},{8,9},{9,8},{10,11... | collective-permute-start | bytes 1572872 | tf_op jit(solution)/shard_map/ppermute | solution.py:571
  28.3 27.0 %collective-permute-start.4 = (bf16[1024,512]{1,0:T(8,128)(2,1)S(1)}, bf16[1024,512]{1,0:T(8,128)(2,1)S(1)}, u32[]{:S(2)}, u32[]{:S(2)}) collective-permute-start(bf16[1024,512]{1,0:T(8,128)(2,1)S(1)} %collective-permute-done.2.b_ref), channel_id=1, source_target_pairs={{0,4},{2,6},{4,0},{6,2},{8,12},{10,14},{12,8},{14,10},{1,5},{3,7},... | collective-permute-start | bytes 3145736 | tf_op jit(solution)/shard_map/ppermute | solution.py:648
  33.0 22.4 %collective-permute-start.5 = (bf16[1024,512]{1,0:T(8,128)(2,1)}, bf16[1024,512]{1,0:T(8,128)(2,1)}, u32[]{:S(2)}, u32[]{:S(2)}) collective-permute-start(bf16[1024,512]{1,0:T(8,128)(2,1)} %collective-permute-done.1.refs_1_), channel_id=1, source_target_pairs={{4,8},{6,10},{8,4},{10,6},{5,9},{7,11},{9,5},{11,7},{20,24},{22,26... | collective-permute-start | bytes 3145736 | tf_op jit(solution)/shard_map/ppermute | solution.py:651
  38.3 15.8 %collective-permute-start.8 = (f32[512,256]{1,0:T(8,128)}, f32[512,256]{1,0:T(8,128)S(1)}, u32[]{:S(2)}, u32[]{:S(2)}) collective-permute-start(f32[512,256]{1,0:T(8,128)} %get-tuple-element.194), channel_id=1, source_target_pairs={{0,1},{1,0},{2,3},{3,2},{4,5},{5,4},{6,7},{7,6},{8,9},{9,8},{10,11... | collective-permute-start | bytes 1572872 | tf_op jit(solution)/shard_map/ppermute | solution.py:571
  55.4 25.7 %collective-permute-start.10 = (bf16[1024,512]{1,0:T(8,128)(2,1)}, bf16[1024,512]{1,0:T(8,128)(2,1)}, u32[]{:S(2)}, u32[]{:S(2)}) collective-permute-start(bf16[1024,512]{1,0:T(8,128)(2,1)} %collective-permute-done.5.c_ref), channel_id=1, source_target_pairs={{0,4},{2,6},{4,0},{6,2},{8,12},{10,14},{12,8},{14,10},{1,5},{3,7},... | collective-permute-start | bytes 3145736 | tf_op jit(solution)/shard_map/ppermute | solution.py:648
  59.3 23.5 %collective-permute-start.9 = (bf16[1024,512]{1,0:T(8,128)(2,1)}, bf16[1024,512]{1,0:T(8,128)(2,1)}, u32[]{:S(2)}, u32[]{:S(2)}) collective-permute-start(bf16[1024,512]{1,0:T(8,128)(2,1)} %collective-permute-done.1.refs_1_), channel_id=1, source_target_pairs={{0,2},{2,0},{4,6},{6,4},{8,10},{10,8},{12,14},{14,12},{1,3},{3,1},... | collective-permute-start | bytes 3145736 | tf_op jit(solution)/shard_map/ppermute | solution.py:654
  60.8 22.0 %collective-permute-start.11 = (bf16[1024,512]{1,0:T(8,128)(2,1)}, bf16[1024,512]{1,0:T(8,128)(2,1)}, u32[]{:S(2)}, u32[]{:S(2)}) collective-permute-start(bf16[1024,512]{1,0:T(8,128)(2,1)} %collective-permute-done.1.refs_1_), channel_id=1, source_target_pairs={{0,1},{1,0},{2,3},{3,2},{4,5},{5,4},{6,7},{7,6},{8,9},{9,8},{10,11... | collective-permute-start | bytes 3145736 | tf_op jit(solution)/shard_map/ppermute | solution.py:571
  60.8 25.9 %collective-permute-start.17 = (bf16[1024,1024]{1,0:T(8,128)(2,1)}, bf16[1024,1024]{1,0:T(8,128)(2,1)}, u32[]{:S(2)}, u32[]{:S(2)}) collective-permute-start(bf16[1024,1024]{1,0:T(8,128)(2,1)} %collective-permute-done.refs_1_.refs_3_), channel_id=1, source_target_pairs={{0,1},{1,0},{2,3},{3,2},{4,5},{5,4},{6,7},{7,6},{8,9},{9,8},{10,11... | collective-permute-start | bytes 6291464 | tf_op jit(solution)/shard_map/ppermute | solution.py:571
  61.3 21.5 %collective-permute-start.12 = (bf16[1024,384]{1,0:T(8,128)(2,1)}, bf16[1024,384]{1,0:T(8,128)(2,1)}, u32[]{:S(2)}, u32[]{:S(2)}) collective-permute-start(bf16[1024,384]{1,0:T(8,128)(2,1)} %slice.52), channel_id=1, source_target_pairs={{4,8},{6,10},{8,4},{10,6},{5,9},{7,11},{9,5},{11,7},{20,24},{22,26... | collective-permute-start | bytes 2359304 | tf_op jit(solution)/shard_map/ppermute | solution.py:651
  82.9 22.6 %collective-permute-start.13 = (bf16[2048,256]{1,0:T(8,128)(2,1)S(1)}, bf16[2048,256]{1,0:T(8,128)(2,1)S(1)}, u32[]{:S(2)}, u32[]{:S(2)}) collective-permute-start(bf16[2048,256]{1,0:T(8,128)(2,1)S(1)} %get-tuple-element.202.refs_2_), channel_id=1, source_target_pairs={{0,2},{2,0},{4,6},{6,4},{8,10},{10,8},{12,14},{14,12},{1,3},{3,1},... | collective-permute-start | bytes 3145736 | tf_op jit(solution)/shard_map/ppermute | solution.py:654
  84.4 21.1 %collective-permute-start.15 = (bf16[2048,256]{1,0:T(8,128)(2,1)S(1)}, bf16[2048,256]{1,0:T(8,128)(2,1)S(1)}, u32[]{:S(2)}, u32[]{:S(2)}) collective-permute-start(bf16[2048,256]{1,0:T(8,128)(2,1)S(1)} %get-tuple-element.202.refs_2_), channel_id=1, source_target_pairs={{0,1},{1,0},{2,3},{3,2},{4,5},{5,4},{6,7},{7,6},{8,9},{9,8},{10,11... | collective-permute-start | bytes 3145736 | tf_op jit(solution)/shard_map/ppermute | solution.py:571
  84.4 21.1 %collective-permute-start.16 = (bf16[1024,512]{1,0:T(8,128)(2,1)}, bf16[1024,512]{1,0:T(8,128)(2,1)S(1)}, u32[]{:S(2)}, u32[]{:S(2)}) collective-permute-start(bf16[1024,512]{1,0:T(8,128)(2,1)} %collective-permute-done.9.refs_4_), channel_id=1, source_target_pairs={{0,1},{1,0},{2,3},{3,2},{4,5},{5,4},{6,7},{7,6},{8,9},{9,8},{10,11... | collective-permute-start | bytes 3145736 | tf_op jit(solution)/shard_map/ppermute | solution.py:571
  84.9 19.7 %collective-permute-start.14 = (bf16[1024,384]{1,0:T(8,128)(2,1)}, bf16[1024,384]{1,0:T(8,128)(2,1)S(1)}, u32[]{:S(2)}, u32[]{:S(2)}) collective-permute-start(bf16[1024,384]{1,0:T(8,128)(2,1)} %slice.52), channel_id=1, source_target_pairs={{0,4},{2,6},{4,0},{6,2},{8,12},{10,14},{12,8},{14,10},{1,5},{3,7},... | collective-permute-start | bytes 2359304 | tf_op jit(solution)/shard_map/ppermute | solution.py:648
  105.6 25.6 %collective-permute-start.18 = (bf16[2048,256]{1,0:T(8,128)(2,1)S(1)}, bf16[2048,256]{1,0:T(8,128)(2,1)S(1)}, u32[]{:S(2)}, u32[]{:S(2)}) collective-permute-start(bf16[2048,256]{1,0:T(8,128)(2,1)S(1)} %get-tuple-element.218.refs_2_), channel_id=1, source_target_pairs={{0,2},{2,0},{4,6},{6,4},{8,10},{10,8},{12,14},{14,12},{1,3},{3,1},... | collective-permute-start | bytes 3145736 | tf_op jit(solution)/shard_map/ppermute | solution.py:654
  107.2 24.0 %collective-permute-start.22 = (bf16[2048,256]{1,0:T(8,128)(2,1)S(1)}, bf16[2048,256]{1,0:T(8,128)(2,1)S(1)}, u32[]{:S(2)}, u32[]{:S(2)}) collective-permute-start(bf16[2048,256]{1,0:T(8,128)(2,1)S(1)} %get-tuple-element.218.refs_2_), channel_id=1, source_target_pairs={{0,1},{1,0},{2,3},{3,2},{4,5},{5,4},{6,7},{7,6},{8,9},{9,8},{10,11... | collective-permute-start | bytes 3145736 | tf_op jit(solution)/shard_map/ppermute | solution.py:571
  107.3 20.0 %collective-permute-start.19 = (bf16[1024,384]{1,0:T(8,128)(2,1)}, bf16[1024,384]{1,0:T(8,128)(2,1)S(1)}, u32[]{:S(2)}, u32[]{:S(2)}) collective-permute-start(bf16[1024,384]{1,0:T(8,128)(2,1)} %collective-permute-done.12.b_ref), channel_id=1, source_target_pairs={{0,4},{2,6},{4,0},{6,2},{8,12},{10,14},{12,8},{14,10},{1,5},{3,7},... | collective-permute-start | bytes 2359304 | tf_op jit(solution)/shard_map/ppermute | solution.py:648
  108.8 18.5 %collective-permute-start.20 = (bf16[1024,384]{1,0:T(8,128)(2,1)S(1)}, bf16[1024,384]{1,0:T(8,128)(2,1)S(1)}, u32[]{:S(2)}, u32[]{:S(2)}) collective-permute-start(bf16[1024,384]{1,0:T(8,128)(2,1)S(1)} %collective-permute-done.14.refs_0_), channel_id=1, source_target_pairs={{4,8},{6,10},{8,4},{10,6},{5,9},{7,11},{9,5},{11,7},{20,24},{22,26... | collective-permute-start | bytes 2359304 | tf_op jit(solution)/shard_map/ppermute | solution.py:651
  131.2 20.0 %collective-permute-start.23 = (bf16[1024,384]{1,0:T(8,128)(2,1)S(1)}, bf16[1024,384]{1,0:T(8,128)(2,1)S(1)}, u32[]{:S(2)}, u32[]{:S(2)}) collective-permute-start(bf16[1024,384]{1,0:T(8,128)(2,1)S(1)} %collective-permute-done.14.refs_0_), channel_id=1, source_target_pairs={{0,2},{2,0},{4,6},{6,4},{8,10},{10,8},{12,14},{14,12},{1,3},{3,1},... | collective-permute-start | bytes 2359304 | tf_op jit(solution)/shard_map/ppermute | solution.py:654
  132.8 19.6 %collective-permute-start.24 = (bf16[1024,384]{1,0:T(8,128)(2,1)S(1)}, bf16[1024,384]{1,0:T(8,128)(2,1)S(1)}, u32[]{:S(2)}, u32[]{:S(2)}) collective-permute-start(bf16[1024,384]{1,0:T(8,128)(2,1)S(1)} %collective-permute-done.20.c_ref), channel_id=1, source_target_pairs={{0,4},{2,6},{4,0},{6,2},{8,12},{10,14},{12,8},{14,10},{1,5},{3,7},... | collective-permute-start | bytes 2359304 | tf_op jit(solution)/shard_map/ppermute | solution.py:648
  134.3 18.1 %collective-permute-start.27 = (bf16[1024,384]{1,0:T(8,128)(2,1)S(1)}, bf16[1024,384]{1,0:T(8,128)(2,1)S(1)}, u32[]{:S(2)}, u32[]{:S(2)}) collective-permute-start(bf16[1024,384]{1,0:T(8,128)(2,1)S(1)} %collective-permute-done.14.refs_0_), channel_id=1, source_target_pairs={{0,1},{1,0},{2,3},{3,2},{4,5},{5,4},{6,7},{7,6},{8,9},{9,8},{10,11... | collective-permute-start | bytes 2359304 | tf_op jit(solution)/shard_map/ppermute | solution.py:571
  134.3 14.3 %collective-permute-start.26 = (bf16[512,512]{1,0:T(8,128)(2,1)S(1)}, bf16[512,512]{1,0:T(8,128)(2,1)S(1)}, u32[]{:S(2)}, u32[]{:S(2)}) collective-permute-start(bf16[512,512]{1,0:T(8,128)(2,1)S(1)} %get-tuple-element.232.refs_0_), channel_id=1, source_target_pairs={{0,16},{16,0},{1,17},{17,1},{2,18},{18,2},{3,19},{19,3},{4,20},{20... | collective-permute-start | bytes 1572872 | tf_op jit(solution)/shard_map/ppermute | solution.py:567
  157.1 24.8 %collective-permute-start.35 = (f32[512,512]{1,0:T(8,128)S(1)}, f32[512,512]{1,0:T(8,128)S(1)}, u32[]{:S(2)}, u32[]{:S(2)}) collective-permute-start(f32[512,512]{1,0:T(8,128)S(1)} %get-tuple-element.260.refs_0_), channel_id=1, source_target_pairs={{0,16},{16,0},{1,17},{17,1},{2,18},{18,2},{3,19},{19,3},{4,20},{20... | collective-permute-start | bytes 3145736 | tf_op jit(solution)/shard_map/ppermute | solution.py:567
  168.2 28.9 %collective-permute-start.36 = (bf16[2064,256]{1,0:T(8,128)(2,1)S(1)}, bf16[2064,256]{1,0:T(8,128)(2,1)S(1)}, u32[]{:S(2)}, u32[]{:S(2)}) collective-permute-start(bf16[2064,256]{1,0:T(8,128)(2,1)S(1)} %get-tuple-element.283.refs_0_), channel_id=1, source_target_pairs={{0,2},{2,0},{4,6},{6,4},{8,10},{10,8},{12,14},{14,12},{1,3},{3,1},... | collective-permute-start | bytes 3170312 | tf_op jit(solution)/shard_map/ppermute | solution.py:654
  181.9 15.1 %collective-permute-start.37 = (bf16[2048,128]{1,0:T(8,128)(2,1)S(1)}, bf16[2048,128]{1,0:T(8,128)(2,1)S(1)}, u32[]{:S(2)}, u32[]{:S(2)}) collective-permute-start(bf16[2048,128]{1,0:T(8,128)(2,1)S(1)} %collective-permute-done.29.b_ref), channel_id=1, source_target_pairs={{0,4},{2,6},{4,0},{6,2},{8,12},{10,14},{12,8},{14,10},{1,5},{3,7},... | collective-permute-start | bytes 1572872 | tf_op jit(solution)/shard_map/ppermute | solution.py:648
  197.2 14.3 %collective-permute-start.40 = (bf16[2048,128]{1,0:T(8,128)(2,1)S(1)}, bf16[2048,128]{1,0:T(8,128)(2,1)S(1)}, u32[]{:S(2)}, u32[]{:S(2)}) collective-permute-start(bf16[2048,128]{1,0:T(8,128)(2,1)S(1)} %collective-permute-done.30.c_ref), channel_id=1, source_target_pairs={{0,4},{2,6},{4,0},{6,2},{8,12},{10,14},{12,8},{14,10},{1,5},{3,7},... | collective-permute-start | bytes 1572872 | tf_op jit(solution)/shard_map/ppermute | solution.py:648
  213.1 14.8 %collective-permute-start.47 = (bf16[512,512]{1,0:T(8,128)(2,1)S(1)}, bf16[512,512]{1,0:T(8,128)(2,1)S(1)}, u32[]{:S(2)}, u32[]{:S(2)}) collective-permute-start(bf16[512,512]{1,0:T(8,128)(2,1)S(1)} %get-tuple-element.309.refs_0_), channel_id=1, source_target_pairs={{0,16},{16,0},{1,17},{17,1},{2,18},{18,2},{3,19},{19,3},{4,20},{20... | collective-permute-start | bytes 1572872 | tf_op jit(solution)/shard_map/ppermute | solution.py:567
  248.8 27.4 %collective-permute-start.55 = (f32[512,512]{1,0:T(8,128)S(1)}, f32[512,512]{1,0:T(8,128)S(1)}, u32[]{:S(2)}, u32[]{:S(2)}) collective-permute-start(f32[512,512]{1,0:T(8,128)S(1)} %get-tuple-element.353), channel_id=1, source_target_pairs={{0,1},{1,0},{2,3},{3,2},{4,5},{5,4},{6,7},{7,6},{8,9},{9,8},{10,11... | collective-permute-start | bytes 3145736 | tf_op jit(solution)/shard_map/ppermute | solution.py:571
  249.1 27.1 %collective-permute-start.56 = (bf16[512,1024]{1,0:T(8,128)(2,1)S(1)}, bf16[512,1024]{1,0:T(8,128)(2,1)S(1)}, u32[]{:S(2)}, u32[]{:S(2)}) collective-permute-start(bf16[512,1024]{1,0:T(8,128)(2,1)S(1)} %copy-done.16), channel_id=1, source_target_pairs={{0,16},{16,0},{1,17},{17,1},{2,18},{18,2},{3,19},{19,3},{4,20},{20... | collective-permute-start | bytes 3145736 | tf_op jit(solution)/shard_map/ppermute | solution.py:567
  (73 other events, 689.8 us)
